TPU v7x, 128 devices: a whole 4x4x4 slice. The times are simulated.
128 devices in a mesh: snd: 8 (over z, core), tile: 16 (over x, y).
Axes of the slice: x: 4, y: 4, z: 4, core: 2. Of those that a mesh axis runs over, the one named last changes fastest.
Arguments:
- level_set: float32 [128, 30720], P('tile'), may hold values from -6 to 6
- tile_home: int32 [128], replicated, may hold values from 0 to 127, as said below
- footprints: int32 [128, 16], P(('snd', 'tile')), may hold values from 0 to 127, as said below
- adjoint_source: bfloat16 [128, 48, 4096], P(('snd', 'tile')), may hold values from -6 to 6
- primal_fields: bfloat16 [128, 3, 48, 4096], P(('snd', 'tile')), may hold values from -6 to 6
Outputs:
- level_grad: float32 [128, 30720], P('tile')
- level_next: float32 [128, 30720], P('tile')
Inputs may be any that keep to these rules, and one draw needn't show every extreme that they name: A permutation: tile g is stored in row tile_home[g] of level_set, on index tile_home[g] // 8 of tile. `footprints`: the 16 tiles of one sounding are distinct; for each index of tile, either none or exactly two of them are stored there.
All inputs are finite; a program needn't handle non-finite values. Where the computation divides by a largest or mean magnitude, that divisor is 1e-20 or more.
Results may differ from a plain program's by a relative error of at most 0.0003.
Values sent between devices are 32-bit elements; how exact they have to be, the bound alone decides.
A program may use at most 64 MiB of HBM per device.

v0:
```python
import jax
import jax.numpy as jnp
from jax import lax
from jax.sharding import PartitionSpec as P

TX = 16
DEPTH = 48
FOOT = 4
JACOBI = 8


log_low = -1.2
log_span = 2.5
front_width = 0.5
step_size = 0.5


def neighbours(values, mesh_side):
    batch, layers, plane = values.shape
    column = jnp.arange(plane) % mesh_side
    zero_layer = jnp.zeros((batch, 1, plane), jnp.float32)
    result = jnp.concatenate([zero_layer, values[:, :-1]], axis=1) + jnp.concatenate(
        [values[:, 1:], zero_layer], axis=1
    )
    zero_rows = jnp.zeros((batch, layers, mesh_side), jnp.float32)
    result = result + jnp.concatenate([zero_rows, values[:, :, :-mesh_side]], axis=2)
    result = result + jnp.concatenate([values[:, :, mesh_side:], zero_rows], axis=2)
    zero_col = jnp.zeros((batch, layers, 1), jnp.float32)
    western = jnp.where(column != 0, jnp.concatenate([zero_col, values[:, :, :-1]], axis=2), 0.0)
    eastern = jnp.where(
        column != mesh_side - 1, jnp.concatenate([values[:, :, 1:], zero_col], axis=2), 0.0
    )
    return result + western + eastern


def jacobi_solve(source, inverse_diag, mesh_side):
    iterate = jnp.zeros(source.shape, jnp.float32)
    for sweep_index in range(JACOBI):
        iterate = (source + neighbours(iterate, mesh_side)) * inverse_diag
    return iterate


def sensitivity(phi_field, sources, primals, mesh_side):
    smooth = jnp.tanh(phi_field / front_width)
    conduct = jnp.exp(log_low + 0.5 * log_span * (1.0 + smooth))
    slope_term = conduct * (0.5 * log_span / front_width) * (1.0 - smooth * smooth)
    inverse_diag = 1.0 / (6.0 + conduct)
    adjoint_two = jacobi_solve(sources.astype(jnp.float32), inverse_diag, mesh_side)
    adjoint_one = jacobi_solve(conduct * adjoint_two, inverse_diag, mesh_side)
    fields = primals.astype(jnp.float32)
    return -slope_term * (
        adjoint_two * (fields[:, 2] - fields[:, 1]) + adjoint_one * (fields[:, 1] - fields[:, 0])
    )


def to_footprint(entries, block_size):
    shaped = entries.reshape(block_size, FOOT, FOOT, DEPTH, TX, TX)
    return shaped.transpose(0, 3, 1, 4, 2, 5).reshape(block_size, DEPTH, FOOT * TX * FOOT * TX)


def to_entries(footprint_field, block_size):
    shaped = footprint_field.reshape(block_size, DEPTH, FOOT, TX, FOOT, TX)
    return shaped.transpose(0, 2, 4, 1, 3, 5).reshape(block_size * FOOT * FOOT, DEPTH * TX * TX)


def widen(top_part, full_cells):
    lower = jnp.zeros((top_part.shape[0], full_cells - top_part.shape[1]), jnp.float32)
    return jnp.concatenate([top_part, lower], axis=1)


def block_gradient(top_level, tile_home, footprints, adjoint_source, primal_fields, block_size):
    owners = lax.axis_size("tile")
    tile_rows = top_level.shape[0]
    cell_count = top_level.shape[1]
    mesh_side = FOOT * TX
    capacity = 2 * block_size
    tile_ids = footprints.reshape(-1)
    stored = jnp.take(tile_home, tile_ids, axis=0)
    target = stored // tile_rows
    local_row = stored % tile_rows
    order_index = jnp.arange(tile_ids.shape[0])
    earlier = (target[:, None] == target[None, :]) & (order_index[None, :] < order_index[:, None])
    ranking = jnp.sum(earlier.astype(jnp.int32), axis=1)
    slot_index = target * capacity + ranking
    requests = (
        jnp.full((owners * capacity,), -1, jnp.int32)
        .at[slot_index]
        .set(local_row)
        .reshape(owners, capacity)
    )
    asked_rows = lax.all_to_all(requests, "tile", split_axis=0, concat_axis=0, tiled=True)
    picked = jnp.take(top_level, jnp.maximum(asked_rows, 0), axis=0)
    picked = jnp.where((asked_rows >= 0)[:, :, None], picked, 0.0)
    returned = lax.all_to_all(picked, "tile", split_axis=0, concat_axis=0, tiled=True)
    entries = jnp.take(returned.reshape(owners * capacity, cell_count), slot_index, axis=0)
    phi_field = to_footprint(entries, block_size)
    gradient = to_entries(
        sensitivity(phi_field, adjoint_source, primal_fields, mesh_side), block_size
    )
    outgoing = jnp.zeros((owners * capacity, cell_count), jnp.float32).at[slot_index].set(gradient)
    incoming = lax.all_to_all(
        outgoing.reshape(owners, capacity, cell_count),
        "tile",
        split_axis=0,
        concat_axis=0,
        tiled=True,
    )
    selector = (asked_rows.reshape(-1)[None, :] == jnp.arange(tile_rows)[:, None]).astype(
        jnp.float32
    )
    return jnp.dot(
        selector,
        incoming.reshape(owners * capacity, cell_count),
        precision=lax.Precision.HIGHEST,
        preferred_element_type=jnp.float32,
    )


def shards(level_set, tile_home, footprints, adjoint_source, primal_fields):
    sound_count = footprints.shape[0]
    full_cells = level_set.shape[1]
    top_cells = DEPTH * TX * TX
    top_level = level_set[:, :top_cells]
    block_spans = (0, sound_count)
    block_start, block_size = block_spans
    owned_grad = block_gradient(
        top_level, tile_home, footprints, adjoint_source, primal_fields, block_size
    )
    summed = lax.psum(owned_grad, "snd")
    largest = lax.pmax(jnp.max(jnp.abs(summed)), "tile")
    full_grad = widen(summed, full_cells)
    return (full_grad, level_set - step_size * full_grad / (largest + 1e-06))


def solution(mesh):
    return jax.shard_map(
        shards,
        mesh=mesh,
        in_specs=(
            P("tile", None),
            P(),
            P(("snd", "tile"), None),
            P(("snd", "tile"), None, None),
            P(("snd", "tile"), None, None, None),
        ),
        out_specs=(P("tile", None), P("tile", None)),
        check_vma=False,
    )
```

profile of v0, /device:TPU:0, one launch (start us, length us, event | category | flops | bytes accessed | tf_op | source)
XLA Modules:
  0.0 308.0 jit_solution(1622678732324372350)
XLA Ops:
  13.3 7.1 %all-to-all-start = ((s32[16,1,2]{2,1,0:T(1,128)}), s32[16,1,2]{2,1,0:T(1,128)S(1)}, u32[]{:S(2)}, u32[]{:S(2)}) async-start(s32[16,1,2]{2,1,0:T(1,128)} %bitcast.8), calls=%async_computation | async-start | bytes 16384 | tf_op jit(solution)/shard_map/all_to_all | solution.py:91
  20.4 7.5 %all-to-all-done = s32[16,1,2]{2,1,0:T(1,128)S(1)} async-done(((s32[16,1,2]{2,1,0:T(1,128)}), s32[16,1,2]{2,1,0:T(1,128)S(1)}, u32[]{:S(2)}, u32[]{:S(2)}) %all-to-all-start) | async-done | bytes 160 | tf_op jit(solution)/shard_map/all_to_all | solution.py:91
  30.5 2.3 select_select_fusion
  32.8 5.1 %all-to-all-start.1 = ((f32[16,2,12288]{2,1,0:T(2,128)}), f32[16,2,12288]{2,1,0:T(2,128)}, u32[]{:S(2)}, u32[]{:S(2)}) async-start(f32[16,2,12288]{2,1,0:T(2,128)} %select_select_fusion), calls=%async_computation.1 | async-start | bytes 3145728 | tf_op jit(solution)/shard_map/all_to_all | solution.py:94
  38.7 2.7 copy.52
  41.4 5.0 %convert_element_type.12 = f32[1,3,48,4096]{2,3,1,0:T(8,128)} convert(bf16[1,3,48,4096]{2,3,1,0:T(8,128)(2,1)} %copy.52) | non-fusion elementwise | flops 589824 | bytes 3538944 | tf_op jit(solution)/shard_map/convert_element_type | solution.py:50
  46.5 13.9 %all-to-all-done.1 = f32[16,2,12288]{2,1,0:T(2,128)} async-done(((f32[16,2,12288]{2,1,0:T(2,128)}), f32[16,2,12288]{2,1,0:T(2,128)}, u32[]{:S(2)}, u32[]{:S(2)}) %all-to-all-start.1) | async-done | bytes 1572896 | tf_op jit(solution)/shard_map/all_to_all | solution.py:94
  60.3 2.4 reshape.440
  63.6 3.9 %gather.26 = f32[1,4,4,48,16,16]{5,4,3,2,1,0:T(8,128)} reshape(f32[16,12288]{1,0:T(8,128)S(1)} %gather_fusion.2) | data formatting | bytes 1572864 | tf_op jit(solution)/shard_map/jit(_take)/gather | solution.py:95
  67.5 4.6 %copy.48 = f32[1,4,4,48,16,16]{3,5,4,2,1,0:T(8,128)S(1)} copy(f32[1,4,4,48,16,16]{5,4,3,2,1,0:T(8,128)} %gather.26) | data formatting | bytes 1572864 | tf_op jit(solution)/shard_map/jit(_take)/gather | solution.py:95
  72.1 2.2 subtract_bitcast_fusion
  74.6 2.6 fusion
  78.5 3.8 %fusion.1 = f32[1,48,4096]{1,2,0:T(8,128)S(1)} fusion(bf16[1,48,4096]{1,2,0:T(8,128)(2,1)S(1)} %copy.51, f32[1,48,4095]{1,2,0:T(8,128)S(1)} %get-tuple-element.92, f32[1,48,4095]{1,2,0:T(8,128)S(1)} %get-tuple-element.91, f32[1,48,4032]{1,2,0:T(8,128)S(1)} %get-tuple-element.90, f32[1,48,4032]{1,2,0:T(8,128)S(1)} %get-tuple-element.89, ...), kind=kLoop, calls=%fused_computation.14 | loop fusion | flops 2359296 | bytes 6635136 | tf_op jit(solution)/shard_map/mul | solution.py:39
  83.5 3.8 %fusion.2 = f32[1,48,4096]{1,2,0:T(8,128)S(1)} fusion(bf16[1,48,4096]{1,2,0:T(8,128)(2,1)S(1)} %copy.51, f32[1,48,4095]{1,2,0:T(8,128)S(1)} %get-tuple-element.86, f32[1,48,4095]{1,2,0:T(8,128)S(1)} %get-tuple-element.85, f32[1,48,4032]{1,2,0:T(8,128)S(1)} %get-tuple-element.84, f32[1,48,4032]{1,2,0:T(8,128)S(1)} %get-tuple-element.83, ...), kind=kLoop, calls=%fused_computation.15 | loop fusion | flops 2359296 | bytes 6635136 | tf_op jit(solution)/shard_map/mul | solution.py:39
  88.5 3.9 %fusion.3 = f32[1,48,4096]{1,2,0:T(8,128)S(1)} fusion(bf16[1,48,4096]{1,2,0:T(8,128)(2,1)S(1)} %copy.51, f32[1,48,4095]{1,2,0:T(8,128)S(1)} %get-tuple-element.80, f32[1,48,4095]{1,2,0:T(8,128)S(1)} %get-tuple-element.79, f32[1,48,4032]{1,2,0:T(8,128)S(1)} %get-tuple-element.78, f32[1,48,4032]{1,2,0:T(8,128)S(1)} %get-tuple-element.77, ...), kind=kLoop, calls=%fused_computation.16 | loop fusion | flops 2359296 | bytes 6635136 | tf_op jit(solution)/shard_map/mul | solution.py:39
  93.6 3.8 %fusion.4 = f32[1,48,4096]{1,2,0:T(8,128)S(1)} fusion(bf16[1,48,4096]{1,2,0:T(8,128)(2,1)S(1)} %copy.51, f32[1,48,4095]{1,2,0:T(8,128)S(1)} %get-tuple-element.74, f32[1,48,4095]{1,2,0:T(8,128)S(1)} %get-tuple-element.73, f32[1,48,4032]{1,2,0:T(8,128)S(1)} %get-tuple-element.72, f32[1,48,4032]{1,2,0:T(8,128)S(1)} %get-tuple-element.71, ...), kind=kLoop, calls=%fused_computation.17 | loop fusion | flops 2359296 | bytes 6635136 | tf_op jit(solution)/shard_map/mul | solution.py:39
  98.6 3.8 %fusion.5 = f32[1,48,4096]{1,2,0:T(8,128)S(1)} fusion(bf16[1,48,4096]{1,2,0:T(8,128)(2,1)S(1)} %copy.51, f32[1,48,4095]{1,2,0:T(8,128)S(1)} %get-tuple-element.68, f32[1,48,4095]{1,2,0:T(8,128)S(1)} %get-tuple-element.67, f32[1,48,4032]{1,2,0:T(8,128)S(1)} %get-tuple-element.66, f32[1,48,4032]{1,2,0:T(8,128)S(1)} %get-tuple-element.65, ...), kind=kLoop, calls=%fused_computation.18 | loop fusion | flops 2359296 | bytes 6635136 | tf_op jit(solution)/shard_map/mul | solution.py:39
  103.6 3.8 %fusion.6 = f32[1,48,4096]{1,2,0:T(8,128)S(1)} fusion(bf16[1,48,4096]{1,2,0:T(8,128)(2,1)S(1)} %copy.51, f32[1,48,4095]{1,2,0:T(8,128)S(1)} %get-tuple-element.62, f32[1,48,4095]{1,2,0:T(8,128)S(1)} %get-tuple-element.61, f32[1,48,4032]{1,2,0:T(8,128)S(1)} %get-tuple-element.60, f32[1,48,4032]{1,2,0:T(8,128)S(1)} %get-tuple-element.59, ...), kind=kLoop, calls=%fused_computation.19 | loop fusion | flops 2359296 | bytes 6635136 | tf_op jit(solution)/shard_map/mul | solution.py:39
  108.6 4.7 %add_multiply_fusion.6 = (f32[1,48,4096]{1,2,0:T(8,128)S(1)}, f32[1,48,4096]{1,2,0:T(8,128)S(1)}, f32[1,48,4096]{1,2,0:T(8,128)S(1)}) fusion(f32[4096]{0:T(1024)S(1)} %concatenate.289, f32[4096]{0:T(1024)S(1)} %concatenate.287, f32[4096]{0:T(1024)S(1)} %concatenate.285, f32[48]{0:T(128)S(1)} %concatenate.283, pred[4096]{0:T(1024)(128)(4,1)S(1)} %get-tuple-element.98, ...), kind=kLoop, calls=%fused_computation.43 | loop fusion | flops 3735552 | bytes 8257344 | tf_op jit(solution)/shard_map/mul | solution.py:39
  114.6 3.7 %add_multiply_fusion.5 = f32[1,48,4096]{1,2,0:T(8,128)S(1)} fusion(f32[1,48,4096]{1,2,0:T(8,128)S(1)} %get-tuple-element.3, f32[1,48,4095]{1,2,0:T(8,128)S(1)} %get-tuple-element.50, f32[1,48,4095]{1,2,0:T(8,128)S(1)} %get-tuple-element.49, f32[1,48,4032]{1,2,0:T(8,128)S(1)} %get-tuple-element.48, f32[1,48,4032]{1,2,0:T(8,128)S(1)} %get-tuple-element.47, ...), kind=kLoop, calls=%fused_computation.42 | loop fusion | flops 2162688 | bytes 7028352 | tf_op jit(solution)/shard_map/mul | solution.py:39
  119.5 3.7 %add_multiply_fusion.4 = f32[1,48,4096]{1,2,0:T(8,128)S(1)} fusion(f32[1,48,4096]{1,2,0:T(8,128)S(1)} %get-tuple-element.3, f32[1,48,4095]{1,2,0:T(8,128)S(1)} %get-tuple-element.44, f32[1,48,4095]{1,2,0:T(8,128)S(1)} %get-tuple-element.43, f32[1,48,4032]{1,2,0:T(8,128)S(1)} %get-tuple-element.42, f32[1,48,4032]{1,2,0:T(8,128)S(1)} %get-tuple-element.41, ...), kind=kLoop, calls=%fused_computation.41 | loop fusion | flops 2162688 | bytes 7028352 | tf_op jit(solution)/shard_map/mul | solution.py:39
  124.4 3.9 %add_multiply_fusion.3 = f32[1,48,4096]{1,2,0:T(8,128)S(1)} fusion(f32[1,48,4096]{1,2,0:T(8,128)S(1)} %get-tuple-element.3, f32[1,48,4095]{1,2,0:T(8,128)S(1)} %get-tuple-element.38, f32[1,48,4095]{1,2,0:T(8,128)S(1)} %get-tuple-element.37, f32[1,48,4032]{1,2,0:T(8,128)S(1)} %get-tuple-element.36, f32[1,48,4032]{1,2,0:T(8,128)S(1)} %get-tuple-element.35, ...), kind=kLoop, calls=%fused_computation.40 | loop fusion | flops 2162688 | bytes 7028352 | tf_op jit(solution)/shard_map/mul | solution.py:39
  129.5 3.7 %add_multiply_fusion.2 = f32[1,48,4096]{1,2,0:T(8,128)S(1)} fusion(f32[1,48,4096]{1,2,0:T(8,128)S(1)} %get-tuple-element.3, f32[1,48,4095]{1,2,0:T(8,128)S(1)} %get-tuple-element.32, f32[1,48,4095]{1,2,0:T(8,128)S(1)} %get-tuple-element.31, f32[1,48,4032]{1,2,0:T(8,128)S(1)} %get-tuple-element.30, f32[1,48,4032]{1,2,0:T(8,128)S(1)} %get-tuple-element.29, ...), kind=kLoop, calls=%fused_computation.39 | loop fusion | flops 2162688 | bytes 7028352 | tf_op jit(solution)/shard_map/mul | solution.py:39
  134.4 3.7 %add_multiply_fusion.1 = f32[1,48,4096]{1,2,0:T(8,128)S(1)} fusion(f32[1,48,4096]{1,2,0:T(8,128)S(1)} %get-tuple-element.3, f32[1,48,4095]{1,2,0:T(8,128)S(1)} %get-tuple-element.26, f32[1,48,4095]{1,2,0:T(8,128)S(1)} %get-tuple-element.25, f32[1,48,4032]{1,2,0:T(8,128)S(1)} %get-tuple-element.24, f32[1,48,4032]{1,2,0:T(8,128)S(1)} %get-tuple-element.23, ...), kind=kLoop, calls=%fused_computation.38 | loop fusion | flops 2162688 | bytes 7028352 | tf_op jit(solution)/shard_map/mul | solution.py:39
  139.3 3.7 %add_multiply_fusion = f32[1,48,4096]{1,2,0:T(8,128)S(1)} fusion(f32[1,48,4096]{1,2,0:T(8,128)S(1)} %get-tuple-element.3, f32[1,48,4095]{1,2,0:T(8,128)S(1)} %get-tuple-element.20, f32[1,48,4095]{1,2,0:T(8,128)S(1)} %get-tuple-element.19, f32[1,48,4032]{1,2,0:T(8,128)S(1)} %get-tuple-element.18, f32[1,48,4032]{1,2,0:T(8,128)S(1)} %get-tuple-element.17, ...), kind=kLoop, calls=%fused_computation.37 | loop fusion | flops 2162688 | bytes 7028352 | tf_op jit(solution)/shard_map/mul | solution.py:39
  147.1 4.4 %fusion.11 = f32[1,48,4096]{1,2,0:T(8,128)S(1)} fusion(f32[1,3,48,4096]{2,3,1,0:T(8,128)S(1)} %bitcast.107, f32[1,48,4096]{1,2,0:T(8,128)S(1)} %get-tuple-element.4, f32[1,48,4,16,4,16]{1,5,4,3,2,0:T(8,128)S(1)} %copy.50, f32[1,48,4,16,4,16]{1,5,4,3,2,0:T(8,128)S(1)} %copy.49, f32[1,48,4096]{1,2,0:T(8,128)S(1)} %get-tuple-element.3, ...), kind=kLoop, calls=%fused_computation.25 | loop fusion | flops 3932160 | bytes 10960512 | tf_op jit(solution)/shard_map/mul | solution.py:51
  151.5 4.2 %copy.53 = f32[1,4,4,48,16,16]{5,4,3,2,1,0:T(8,128)} copy(f32[1,4,4,48,16,16]{3,5,2,4,1,0:T(8,128)S(1)} %bitcast.108) | data formatting | bytes 1572864 | tf_op jit(solution)/shard_map/transpose | solution.py:63
  155.7 6.9 %reshape.484 = f32[16,12288]{1,0:T(8,128)S(1)} reshape(f32[1,4,4,48,16,16]{5,4,3,2,1,0:T(8,128)} %copy.53) | data formatting | bytes 1572864 | tf_op jit(solution)/shard_map/reshape | solution.py:63
  166.5 3.8 %all-to-all-start.2 = ((f32[16,2,12288]{2,1,0:T(2,128)}), f32[16,2,12288]{2,1,0:T(2,128)S(1)}, u32[]{:S(2)}, u32[]{:S(2)}) async-start(f32[16,2,12288]{2,1,0:T(2,128)} %reshape.443), calls=%async_computation.2 | async-start | bytes 3145728 | tf_op jit(solution)/shard_map/all_to_all | solution.py:101
  171.2 20.0 %all-to-all-done.2 = f32[16,2,12288]{2,1,0:T(2,128)S(1)} async-done(((f32[16,2,12288]{2,1,0:T(2,128)}), f32[16,2,12288]{2,1,0:T(2,128)S(1)}, u32[]{:S(2)}, u32[]{:S(2)}) %all-to-all-start.2) | async-done | bytes 1572896 | tf_op jit(solution)/shard_map/all_to_all | solution.py:101
  193.7 59.9 %all-reduce.91.cloned.1.call-done = f32[8,12288]{1,0:T(8,128)} async-done(((f32[8,12288]{1,0:T(8,128)}), f32[8,12288]{1,0:T(8,128)}) %all-reduce.91.cloned.1.call-update) | async-done | bytes 393232 | tf_op jit(solution)/shard_map/psum | solution.py:129
  255.3 40.9 %pmax.7 = f32[]{:T(128)} all-reduce(f32[]{:T(128)} %abs_reduce_fusion), channel_id=1, replica_groups=mesh['snd'=8,'tile'=16] {'tile'}, use_global_device_ids=true, to_apply=%region_5.6 | all-reduce | flops 1 | bytes 8 | tf_op jit(solution)/shard_map/pmax | solution.py:130
  (117 shorter events, 43.3 us)
Async XLA Ops:
  7.2 0.8 copy-start
  7.2 21.3 %slice-start = ((f32[8,30720]{1,0:T(8,128)}), f32[8,12288]{1,0:T(8,128)S(1)}, s32[]{:S(2)}) async-start(f32[8,30720]{1,0:T(8,128)} %param.5), calls=%async_computation.4 | async-start | bytes 786432 | tf_op jit(solution)/shard_map/slice | solution.py:123
  11.9 34.5 %copy-start.8 = (s32[16]{0:T(128)}, s32[16]{0:T(128)S(1)}, u32[]{:S(2)}) copy-start(s32[16]{0:T(128)S(1)} %fusion.30) | copy-start | bytes 196
  13.3 14.6 %all-to-all-start = ((s32[16,1,2]{2,1,0:T(1,128)}), s32[16,1,2]{2,1,0:T(1,128)S(1)}, u32[]{:S(2)}, u32[]{:S(2)}) async-start(s32[16,1,2]{2,1,0:T(1,128)} %bitcast.8), calls=%async_computation | async-start | bytes 16384 | tf_op jit(solution)/shard_map/all_to_all | solution.py:91
  27.9 0.6 copy-start.6
  32.8 5.3 %copy-start.5 = (bf16[1,48,4096]{2,1,0:T(8,128)(2,1)S(1)}, bf16[1,48,4096]{2,1,0:T(8,128)(2,1)}, u32[]{:S(2)}) copy-start(bf16[1,48,4096]{2,1,0:T(8,128)(2,1)} %param.8) | copy-start | bytes 1179652
  32.8 5.9 %copy-start.4 = (bf16[1,3,48,4096]{3,2,1,0:T(8,128)(2,1)S(1)}, bf16[1,3,48,4096]{3,2,1,0:T(8,128)(2,1)}, u32[]{:S(2)}) copy-start(bf16[1,3,48,4096]{3,2,1,0:T(8,128)(2,1)} %param.9) | copy-start | bytes 3538948
  32.8 27.5 %all-to-all-start.1 = ((f32[16,2,12288]{2,1,0:T(2,128)}), f32[16,2,12288]{2,1,0:T(2,128)}, u32[]{:S(2)}, u32[]{:S(2)}) async-start(f32[16,2,12288]{2,1,0:T(2,128)} %select_select_fusion), calls=%async_computation.1 | async-start | bytes 3145728 | tf_op jit(solution)/shard_map/all_to_all | solution.py:94
  143.6 2.8 slice-start.1
  143.9 1.7 copy-start.3
  143.9 3.2 %slice-start.2 = ((s8[6291456]{0:T(1024)(128)(4,1)}), s8[2097152]{0:T(1024)(128)(4,1)S(1)}, s32[]{:S(2)}) async-start(s8[6291456]{0:T(1024)(128)(4,1)} %bitcast.106), calls=%async_computation.6 | async-start | bytes 4194304
  166.5 3.9 %copy-start.7 = (s32[16,1,2]{2,1,0:T(1,128)S(1)}, s32[16,1,2]{2,1,0:T(1,128)}, u32[]{:S(2)}) copy-start(s32[16,1,2]{2,1,0:T(1,128)} %copy-done.6) | copy-start | bytes 388
  166.5 24.7 %all-to-all-start.2 = ((f32[16,2,12288]{2,1,0:T(2,128)}), f32[16,2,12288]{2,1,0:T(2,128)S(1)}, u32[]{:S(2)}, u32[]{:S(2)}) async-start(f32[16,2,12288]{2,1,0:T(2,128)} %reshape.443), calls=%async_computation.2 | async-start | bytes 3145728 | tf_op jit(solution)/shard_map/all_to_all | solution.py:101
  170.4 83.3 %all-reduce.91.cloned.1.call-start = ((), (), s32[]{:S(2)}) async-start(), calls=%async_computation.3 | async-start | bytes 786432 | tf_op jit(solution)/shard_map/psum | solution.py:129
  192.3 106.6 %copy-start.2 = (f32[8,30720]{1,0:T(8,128)S(1)}, f32[8,30720]{1,0:T(8,128)}, u32[]{:S(2)}) copy-start(f32[8,30720]{1,0:T(8,128)} %param.5) | copy-start | bytes 2949124
  193.7 107.2 %copy-start.1 = (s32[128]{0:T(128)S(1)}, s32[128]{0:T(128)}, u32[]{:S(2)}) copy-start(s32[128]{0:T(128)} %param.6) | copy-start | bytes 1540
Sparse Core Ops, SparseCore 0:
  193.9 59.7 all-reduce.90
where the time goes:
time: 312 us; the launch traced here: 308 us
  waiting for transfers between devices  101 us (32%)
  other arithmetic  74 us (24%)
  local copies, waits for them, and re-layouts  58.6 us (19%)
  blocking collectives  40.9 us (13%)
  starting transfers between devices  16.1 us (5%)
  between operations  15.7 us (5%)
    psum x1, waiting for transfers between devices, shards(): summed = lax.psum(owned_grad, 'snd')  59.9 us
    mul x14, other arithmetic, jacobi_solve(): iterate = (source + neighbours(iterate, mesh_side)) * inverse_diag  52.2 us
    pmax x1, blocking collectives, shards(): largest = lax.pmax(jnp.max(jnp.abs(summed)), 'tile')  40.9 us
    all_to_all x1, waiting for transfers between devices, block_gradient(): lax.all_to_all(outgoing.reshape(owners, capacity, cell_count), 'tile', sp...  20 us
    all_to_all x1, waiting for transfers between devices, block_gradient(): lax.all_to_all(picked, 'tile', split_axis=0, concat_axis=0, tiled=True)  13.9 us
    gather x3, local copies, waits for them, and re-layouts, block_gradient(): jnp.take(returned.reshape(owners * capacity, cell_count), slot_index, axi...  9.31 us
    slice x14, local copies, waits for them, and re-layouts, neighbours(): values[:, :-1]  9.27 us
    all_to_all x1, waiting for transfers between devices, block_gradient(): lax.all_to_all(requests, 'tile', split_axis=0, concat_axis=0, tiled=True)  7.48 us
  transfers between devices with their start and end apart: 4, of which 4 were waited for; matrix products, arithmetic and copies ran while one was open for 3% of the time, Pallas kernels for 0%

commit v1 on v0

v1 whole, which is shorter than its diff:
```python
import functools

import jax
import jax.numpy as jnp
from jax import lax
from jax.experimental import pallas as pl
from jax.experimental.pallas import tpu as pltpu
from jax.sharding import PartitionSpec as P

MESH = pl.DeviceIdType.MESH

TX = 16
DEPTH = 48
FOOT = 4
JACOBI = 8
NTILE = 16
NSND = 8
TDEV = 8
TILES = NTILE * TDEV
ENTRIES = FOOT * FOOT
TOP = DEPTH * TX * TX
SLAB = TOP // NSND
CHUNKS = SLAB // 128
SROWS = CHUNKS * ENTRIES

log_low = -1.2
log_span = 2.5
front_width = 0.5
step_size = 0.5


def exchange_groups(blocks, lane):
    blocks = list(blocks)
    for bit in range(3):
        shift = TX << bit
        low = (lane & shift) == 0
        for i in range(8):
            if i & (1 << bit):
                continue
            j = i | (1 << bit)
            a, b = blocks[i], blocks[j]
            blocks[i] = jnp.where(low, a, pltpu.roll(b, shift, 1))
            blocks[j] = jnp.where(low, pltpu.roll(a, 128 - shift, 1), b)
    return blocks


def split3(x):
    hi = x.astype(jnp.bfloat16)
    rest = x - hi.astype(jnp.float32)
    mid = rest.astype(jnp.bfloat16)
    lo = (rest - mid.astype(jnp.float32)).astype(jnp.bfloat16)
    return hi, mid, lo


def onehot_dot(onehot, x):
    return sum(jnp.dot(onehot, part, preferred_element_type=jnp.float32) for part in split3(x))


def kernel(
    footprints,
    tile_home,
    level_set,
    adjoint_source,
    primal_fields,
    grad_ref,
    peak_ref,
    src_in,
    prim_in,
    gathered,
    request,
    picked,
    returned,
    source,
    diff21,
    diff10,
    conduct,
    inverse,
    slope,
    va,
    vb,
    adjoint_two,
    outgoing,
    arrived,
    partial,
    owned,
    peaks,
    peaks2,
    local_sem,
    ag_send,
    ag_recv,
    rq_send,
    rq_recv,
    pk_send,
    pk_recv,
    og_send,
    og_recv,
    rs_send,
    rs_recv,
    fin_send,
    fin_recv,
    mp_send,
    mp_recv,
    mc_send,
    mc_recv,
):
    snd = lax.axis_index("snd")
    tile = lax.axis_index("tile")
    x, y = tile // 4, tile % 4
    z, core = snd // 2, snd % 2

    plane = []
    for i in range(1, 16):
        dx, dy = i // 4, i % 4
        to = ((x + dx) % 4) * 4 + (y + dy) % 4
        frm = ((x + 4 - dx) % 4) * 4 + (y + 4 - dy) % 4
        plane.append((i, to, frm))
    column = []
    for i in range(1, 8):
        dz, dc = i // 2, i % 2
        to = ((z + dz) % 4) * 2 + (core + dc) % 2
        frm = ((z + 4 - dz) % 4) * 2 + (core + dc) % 2
        column.append((i, to, frm))

    load_src = pltpu.make_async_copy(adjoint_source, src_in, local_sem.at[0])
    load_prim = pltpu.make_async_copy(primal_fields, prim_in, local_sem.at[1])
    own_cells = level_set.at[:, pl.ds(pl.multiple_of(snd * SLAB, SLAB), SLAB)]
    load_own = pltpu.make_async_copy(own_cells, gathered.at[tile], local_sem.at[2])
    load_own.start()
    load_src.start()
    load_prim.start()

    barrier = pltpu.get_barrier_semaphore()
    for _, to, _ in plane:
        pl.semaphore_signal(barrier, inc=1, device_id=(snd, to), device_id_type=MESH)
    for _, to, _ in column:
        pl.semaphore_signal(barrier, inc=1, device_id=(to, tile), device_id_type=MESH)

    wanted_rows = lax.broadcasted_iota(jnp.int32, (ENTRIES, TILES), 0)
    stored_rows = lax.broadcasted_iota(jnp.int32, (ENTRIES, TILES), 1)
    wanted = jnp.zeros((ENTRIES, TILES), jnp.int32)
    for j in range(ENTRIES):
        wanted = jnp.where(wanted_rows == j, tile_home[footprints[0, j]], wanted)
    mine = pl.ds(pl.multiple_of(snd * ENTRIES, ENTRIES), ENTRIES)
    request[mine, :] = jnp.where(wanted == stored_rows, 1.0, 0.0)

    pl.semaphore_wait(barrier, 22)

    ag, rq = [], []
    load_own.wait()
    for i, to, frm in plane:
        copy = pltpu.make_async_remote_copy(
            gathered.at[tile], gathered.at[tile], ag_send.at[i], ag_recv.at[i], (snd, to), MESH
        )
        copy.start()
        ag.append(copy)
    for i, to, frm in column:
        copy = pltpu.make_async_remote_copy(
            request.at[mine], request.at[mine], rq_send.at[i], rq_recv.at[i], (to, tile), MESH
        )
        copy.start()
        rq.append(copy)

    lane = lax.broadcasted_iota(jnp.int32, (DEPTH, 128), 1)
    left = lane < 64

    def halves(top, bottom):
        return (
            jnp.where(left, top, pltpu.roll(bottom, 64, 1)),
            jnp.where(left, pltpu.roll(top, 64, 1), bottom),
        )

    load_src.wait()
    load_prim.wait()

    def lay_out(rp, carry):
        low = pl.ds(pl.multiple_of(rp * 128, 128), 128)
        high = pl.ds(pl.multiple_of(rp * 128 + 2048, 128), 128)
        even, odd = halves(
            src_in[0, :, low].astype(jnp.float32), src_in[0, :, high].astype(jnp.float32)
        )
        source[2 * rp] = even
        source[2 * rp + 1] = odd
        fields = [
            [prim_in[0, k, :, part].astype(jnp.float32) for part in (low, high)] for k in range(3)
        ]
        even, odd = halves(fields[2][0] - fields[1][0], fields[2][1] - fields[1][1])
        diff21[2 * rp] = even
        diff21[2 * rp + 1] = odd
        even, odd = halves(fields[1][0] - fields[0][0], fields[1][1] - fields[0][1])
        diff10[2 * rp] = even
        diff10[2 * rp + 1] = odd
        return carry

    lax.fori_loop(0, 16, lay_out, 0)

    zeros8 = jnp.zeros((34, 8, 128), jnp.float32)
    for buf in (va, vb):
        buf[:, 0:8, :] = zeros8
        buf[:, 56:64, :] = zeros8

    for copy in rq:
        copy.wait()
    for copy in ag:
        copy.wait()
    onehot = request[...]
    pick = onehot.astype(jnp.bfloat16)
    place = onehot.T.astype(jnp.bfloat16)
    for c in range(CHUNKS):
        cells = gathered[:, :, c * 128 : (c + 1) * 128].reshape(TILES, 128)
        picked[:, c * ENTRIES : (c + 1) * ENTRIES, :] = onehot_dot(pick, cells).reshape(
            NSND, ENTRIES, 128
        )
    slab_rows = pl.ds(pl.multiple_of(snd * SROWS, SROWS), SROWS)
    pk = []
    for i, to, frm in column:
        copy = pltpu.make_async_remote_copy(
            picked.at[to], returned.at[slab_rows], pk_send.at[i], pk_recv.at[i], (to, tile), MESH
        )
        copy.start()
        pk.append(copy)
    returned[slab_rows, :] = picked[snd]
    for copy in pk:
        copy.wait()

    lane8 = lax.broadcasted_iota(jnp.int32, (8, 128), 1)

    def block_rows(step, g):
        db, rest = step // 4, step % 4
        th, b1 = rest // 2, rest % 2
        entry = (2 * (g // 4) + b1) * 4 + g % 4
        start = (db * 16 + th) * ENTRIES + entry
        return pl.ds(start, 8, stride=2 * ENTRIES), pl.multiple_of(db * 8, 8), b1 * 16 + th * 8

    def enter(step, carry):
        blocks = []
        for g in range(8):
            rows, depth, row = block_rows(step, g)
            blocks.append(returned[rows, :])
        for q, phi in enumerate(exchange_groups(blocks, lane8)):
            smooth = jnp.tanh(phi / front_width)
            cond = jnp.exp(log_low + 0.5 * log_span * (1.0 + smooth))
            at = pl.ds(depth, 8)
            inv = 1.0 / (6.0 + cond)
            conduct[row + q, at, :] = cond
            inverse[row + q, at, :] = inv
            slope[row + q, at, :] = (
                cond * (0.5 * log_span / front_width) * (1.0 - smooth * smooth)
            )
            va[row + q + 1, pl.ds(depth + 8, 8), :] = source[row + q, at, :] * inv
        return carry

    lax.fori_loop(0, 24, enter, 0)

    col = lane & 63
    not_first = col != 0
    not_last = col != 63

    def edges(buf):
        buf[0, 8:56, :] = jnp.where(left, 0.0, pltpu.roll(buf[32, 8:56, :], 64, 1))
        buf[33, 8:56, :] = jnp.where(left, pltpu.roll(buf[1, 8:56, :], 64, 1), 0.0)

    def relaxed(now, row, rhs):
        v = now[row + 1, 8:56, :]
        total = now[row + 1, 7:55, :] + now[row + 1, 9:57, :]
        total = total + now[row, 8:56, :] + now[row + 2, 8:56, :]
        total = total + jnp.where(not_first, pltpu.roll(v, 1, 1), 0.0)
        total = total + jnp.where(not_last, pltpu.roll(v, 127, 1), 0.0)
        return (rhs[row] + total) * inverse[row]

    def solve(rhs, last):
        now, later = va, vb
        for sweep in range(1, JACOBI):
            edges(now)
            final = sweep == JACOBI - 1

            def body(row, carry, now=now, later=later, final=final):
                value = relaxed(now, row, rhs)
                if final:
                    last(row, value)
                else:
                    later[row + 1, 8:56, :] = value
                return carry

            lax.fori_loop(0, 32, body, 0)
            now, later = later, now

    def keep_two(row, value):
        adjoint_two[row] = value

    solve(source, keep_two)

    def second(row, carry):
        rhs = conduct[row] * adjoint_two[row]
        source[row] = rhs
        va[row + 1, 8:56, :] = rhs * inverse[row]
        return carry

    lax.fori_loop(0, 32, second, 0)

    def gradient(row, value):
        vb[row + 1, 8:56, :] = -slope[row] * (
            adjoint_two[row] * diff21[row] + value * diff10[row]
        )

    solve(source, gradient)

    def leave(step, carry):
        _, depth, row = block_rows(step, 0)
        blocks = [vb[row + q + 1, pl.ds(depth + 8, 8), :] for q in range(8)]
        for g, block in enumerate(exchange_groups(blocks, lane8)):
            rows, _, _ = block_rows(step, g)
            outgoing[rows, :] = block
        return carry

    lax.fori_loop(0, 24, leave, 0)

    og = []
    for i, to, frm in column:
        rows = pl.ds(pl.multiple_of(to * SROWS, SROWS), SROWS)
        copy = pltpu.make_async_remote_copy(
            outgoing.at[rows], arrived.at[snd], og_send.at[i], og_recv.at[i], (to, tile), MESH
        )
        copy.start()
        og.append(copy)
    arrived[snd] = outgoing[slab_rows, :]
    for copy in og:
        copy.wait()
    for c in range(CHUNKS):
        cells = arrived[:, c * ENTRIES : (c + 1) * ENTRIES, :].reshape(TILES, 128)
        partial[:, :, c * 128 : (c + 1) * 128] = onehot_dot(place, cells).reshape(
            NTILE, TDEV, 128
        )

    rs = []
    for i, to, frm in plane:
        copy = pltpu.make_async_remote_copy(
            partial.at[to], owned.at[tile], rs_send.at[i], rs_recv.at[i], (snd, to), MESH
        )
        copy.start()
        rs.append(copy)
    owned[tile] = partial[tile]
    for copy in rs:
        copy.wait()
    slab = owned[0]
    for i in range(1, NTILE):
        slab = slab + owned[i]
    slab_cells = pl.ds(pl.multiple_of(snd * SLAB, SLAB), SLAB)
    grad_ref[:, slab_cells] = slab
    size = jnp.abs(slab)
    top = size[:, 0:128]
    for c in range(1, CHUNKS):
        top = jnp.maximum(top, size[:, c * 128 : (c + 1) * 128])
    peaks[tile] = top

    mp, fin, mc = [], [], []
    for i, to, frm in plane:
        copy = pltpu.make_async_remote_copy(
            peaks.at[tile], peaks.at[tile], mp_send.at[i], mp_recv.at[i], (snd, to), MESH
        )
        copy.start()
        mp.append(copy)
    for i, to, frm in column:
        copy = pltpu.make_async_remote_copy(
            grad_ref.at[:, slab_cells],
            grad_ref.at[:, slab_cells],
            fin_send.at[i],
            fin_recv.at[i],
            (to, tile),
            MESH,
        )
        copy.start()
        fin.append(copy)
    for copy in mp:
        copy.wait()
    top = peaks[0]
    for i in range(1, NTILE):
        top = jnp.maximum(top, peaks[i])
    peaks2[snd] = top
    for i, to, frm in column:
        copy = pltpu.make_async_remote_copy(
            peaks2.at[snd], peaks2.at[snd], mc_send.at[i], mc_recv.at[i], (to, tile), MESH
        )
        copy.start()
        mc.append(copy)
    for copy in mc:
        copy.wait()
    top = peaks2[0]
    for i in range(1, NSND):
        top = jnp.maximum(top, peaks2[i])
    peak_ref[...] = top
    for copy in fin:
        copy.wait()


def finish(grad, peak, level_set, grad_out, next_out):
    scale = step_size / (jnp.max(peak[...]) + 1e-6)
    grad_out[:, 0:TOP] = grad[...]
    next_out[:, 0:TOP] = level_set[:, 0:TOP] - scale * grad[...]
    rest = level_set.shape[1] - TOP
    grad_out[:, TOP:] = jnp.zeros((TDEV, rest), jnp.float32)
    next_out[:, TOP:] = level_set[:, TOP:]


def shards(level_set, tile_home, footprints, adjoint_source, primal_fields):
    f32 = jnp.float32
    smem = pl.BlockSpec(memory_space=pltpu.SMEM)
    anywhere = pl.BlockSpec(memory_space=pl.ANY)
    vmem = pl.BlockSpec(memory_space=pltpu.VMEM)
    field = pltpu.VMEM((32, DEPTH, 128), f32)
    padded = pltpu.VMEM((34, DEPTH + 16, 128), f32)
    dma = pltpu.SemaphoreType.DMA
    grad, peak = pl.pallas_call(
        kernel,
        out_shape=(
            jax.ShapeDtypeStruct((TDEV, TOP), f32),
            jax.ShapeDtypeStruct((8, 128), f32),
        ),
        in_specs=[smem, smem, anywhere, anywhere, anywhere],
        out_specs=(vmem, vmem),
        scratch_shapes=[
            pltpu.VMEM(adjoint_source.shape, jnp.bfloat16),
            pltpu.VMEM(primal_fields.shape, jnp.bfloat16),
            pltpu.VMEM((NTILE, TDEV, SLAB), f32),
            pltpu.VMEM((NSND * ENTRIES, TILES), f32),
            pltpu.VMEM((NSND, SROWS, 128), f32),
            pltpu.VMEM((NSND * SROWS, 128), f32),
            field,
            field,
            field,
            field,
            field,
            field,
            padded,
            padded,
            field,
            pltpu.VMEM((NSND * SROWS, 128), f32),
            pltpu.VMEM((NSND, SROWS, 128), f32),
            pltpu.VMEM((NTILE, TDEV, SLAB), f32),
            pltpu.VMEM((NTILE, TDEV, SLAB), f32),
            pltpu.VMEM((NTILE, 8, 128), f32),
            pltpu.VMEM((NSND, 8, 128), f32),
            dma((3,)),
            dma((16,)),
            dma((16,)),
            dma((8,)),
            dma((8,)),
            dma((8,)),
            dma((8,)),
            dma((8,)),
            dma((8,)),
            dma((16,)),
            dma((16,)),
            dma((8,)),
            dma((8,)),
            dma((16,)),
            dma((16,)),
            dma((8,)),
            dma((8,)),
        ],
        compiler_params=pltpu.CompilerParams(
            collective_id=0, has_side_effects=True, vmem_limit_bytes=40 * 1024 * 1024
        ),
    )(footprints, tile_home, level_set, adjoint_source, primal_fields)
    out = jax.ShapeDtypeStruct(level_set.shape, f32)
    return pl.pallas_call(
        finish,
        out_shape=(out, out),
        in_specs=[vmem, vmem, vmem],
        out_specs=(vmem, vmem),
        compiler_params=pltpu.CompilerParams(vmem_limit_bytes=40 * 1024 * 1024),
    )(grad, peak, level_set)


def solution(mesh):
    return jax.shard_map(
        shards,
        mesh=mesh,
        in_specs=(
            P("tile", None),
            P(),
            P(("snd", "tile"), None),
            P(("snd", "tile"), None, None),
            P(("snd", "tile"), None, None, None),
        ),
        out_specs=(P("tile", None), P("tile", None)),
        check_vma=False,
    )
```

time: 312 us -> 124 us (0.40)
  Pallas kernels: 0 us -> 118 us
  waiting for transfers between devices: 101 us -> 0 us
  other arithmetic: 74 us -> 0 us
  local copies, waits for them, and re-layouts: 58.6 us -> 4.77 us
  blocking collectives: 40.9 us -> 0 us
  starting transfers between devices: 16.1 us -> 0 us
  between operations: 15.7 us -> 0.66 us
    pallas_call x0 -> x2, Pallas kernels: none -> 118 us  [the longest x1 116 us: shards(): pl.pallas_call(kernel, out_shape=(jax.ShapeDtypeStruct((TDEV, TOP), f32),...]
    psum x1 -> x0, waiting for transfers between devices: 59.9 us -> none  [shards(): summed = lax.psum(owned_grad, 'snd')]
    mul x15 -> x0, other arithmetic: 56.6 us -> none  [the longest x14 52.2 us: jacobi_solve(): iterate = (source + neighbours(iterate, mesh_side)) * inverse_diag]
    all_to_all x3 -> x0, waiting for transfers between devices: 41.4 us -> none  [the longest x1 20 us: block_gradient(): lax.all_to_all(outgoing.reshape(owners, capacity, cell_count), 'tile', sp...]
    pmax x1 -> x0, blocking collectives: 40.9 us -> none  [shards(): largest = lax.pmax(jnp.max(jnp.abs(summed)), 'tile')]
    slice x44 -> x0, local copies, waits for them, and re-layouts: 17 us -> none  [the longest x14 9.27 us: neighbours(): values[:, :-1]]
    all_to_all x3 -> x0, starting transfers between devices: 16 us -> none  [the longest x1 7.12 us: block_gradient(): lax.all_to_all(requests, 'tile', split_axis=0, concat_axis=0, tiled=True)]
    reshape x5 -> x0, local copies, waits for them, and re-layouts: 12.6 us -> none  [the longest x1 6.9 us: to_entries(): shaped.transpose(0, 2, 4, 1, 3, 5)]
  transfers between devices with their start and end apart: 4 -> 0, of which waited for: 4 -> 0; matrix products, arithmetic and copies ran while one was open for 3% -> 0% of each run, Pallas kernels for 0% -> 0%
where the time goes in v1:
time: 124 us; the launch traced here: 123 us
  Pallas kernels  118 us (95%)
  local copies, waits for them, and re-layouts  4.77 us (4%)
    pallas_call x1, Pallas kernels, shards(): pl.pallas_call(kernel, out_shape=(jax.ShapeDtypeStruct((TDEV, TOP), f32),...  116 us
    unnamed x12, local copies, waits for them, and re-layouts  4.77 us

profile of v1, /device:TPU:0, one launch (start us, length us, event | category | flops | bytes accessed | tf_op | source)
XLA Modules:
  0.0 123.0 jit_solution(4621610708398555361)
XLA Ops:
  0.6 0.0 copy-start
  0.6 1.2 copy-done
  1.8 0.0 copy-start.2
  1.8 1.3 %copy-done.2 = bf16[1,3,48,4096]{3,2,1,0:T(8,128)(2,1)S(1)} copy-done((bf16[1,3,48,4096]{3,2,1,0:T(8,128)(2,1)S(1)}, bf16[1,3,48,4096]{3,2,1,0:T(8,128)(2,1)}, u32[]{:S(2)}) %copy-start.2) | copy-done | bytes 1179672
  3.1 0.0 copy-start.3
  3.1 1.0 copy-done.3
  4.1 0.0 copy-start.4
  4.1 0.7 copy-done.4
  4.8 0.0 copy-start.5
  4.8 0.7 copy-done.5
  5.4 0.0 copy-start.1
  5.4 116.2 %shard_map.68 = (f32[8,12288]{1,0:T(8,128)S(1)}, f32[8,128]{1,0:T(8,128)S(1)}) custom-call(s32[1,16]{1,0:T(1,128)S(1)} %copy-done.4, s32[128]{0:T(128)S(1)} %copy-done.5, f32[8,30720]{1,0:T(8,128)S(1)} %copy-done, bf16[1,48,4096]{2,1,0:T(8,128)(2,1)S(1)} %copy-done.3, bf16[1,3,48,4096]{3,2,1,0:T(8,128)(2,1)S(1)} %copy-done.2), custom_call_target="tpu_custom_call" | custom-call | tf_op jit(solution)/shard_map/pallas_call | solution.py:412
  121.6 0.0 copy-done.1
  121.6 1.4 %shard_map.69 = (f32[8,30720]{1,0:T(8,128)}, f32[8,30720]{1,0:T(8,128)}) custom-call(f32[8,12288]{1,0:T(8,128)S(1)} %get-tuple-element.4.grad, f32[8,128]{1,0:T(8,128)S(1)} %get-tuple-element.5.peak, f32[8,30720]{1,0:T(8,128)S(1)} %copy-done.1), custom_call_target="tpu_custom_call" | custom-call | tf_op jit(solution)/shard_map/pallas_call | solution.py:465
Async XLA Ops:
  0.6 1.2 copy-start
  1.8 1.3 %copy-start.2 = (bf16[1,3,48,4096]{3,2,1,0:T(8,128)(2,1)S(1)}, bf16[1,3,48,4096]{3,2,1,0:T(8,128)(2,1)}, u32[]{:S(2)}) copy-start(bf16[1,3,48,4096]{3,2,1,0:T(8,128)(2,1)} %primal_fields.1) | copy-start | bytes 3538948
  3.1 1.0 copy-start.3
  4.1 0.7 copy-start.4
  4.8 0.7 copy-start.5
  5.4 116.2 %copy-start.1 = (f32[8,30720]{1,0:T(8,128)S(1)}, f32[8,30720]{1,0:T(8,128)}, u32[]{:S(2)}) copy-start(f32[8,30720]{1,0:T(8,128)} %level_set.3) | copy-start | bytes 2949124

commit v2 on v1

v2 whole, which is shorter than its diff:
```python
import functools

import jax
import jax.numpy as jnp
from jax import lax
from jax.experimental import pallas as pl
from jax.experimental.pallas import tpu as pltpu
from jax.sharding import PartitionSpec as P

MESH = pl.DeviceIdType.MESH

TX = 16
DEPTH = 48
FOOT = 4
JACOBI = 8
NTILE = 16
NSND = 8
TDEV = 8
TILES = NTILE * TDEV
ENTRIES = FOOT * FOOT
TOP = DEPTH * TX * TX
SLAB = TOP // NSND
CHUNKS = SLAB // 128
SROWS = CHUNKS * ENTRIES
PIECES = 3
PCHUNKS = CHUNKS // PIECES
PCELLS = SLAB // PIECES
PROWS = SROWS // PIECES

VMEM_LIMIT = 60 * 1024 * 1024

log_low = -1.2
log_span = 2.5
front_width = 0.5
step_size = 0.5


def exchange_groups(blocks, lane):
    turned = [pltpu.roll(v, TX * g, 1) if g else v for g, v in enumerate(blocks)]
    for bit in range(3):
        step = 1 << bit
        upper = (lane & (TX * step)) != 0
        turned = [jnp.where(upper, turned[(i + step) % 8], turned[i]) for i in range(8)]
    return [pltpu.roll(turned[(8 - q) % 8], 128 - TX * q, 1) if q else turned[0] for q in range(8)]


def split3(x):
    hi = x.astype(jnp.bfloat16)
    rest = x - hi.astype(jnp.float32)
    mid = rest.astype(jnp.bfloat16)
    lo = (rest - mid.astype(jnp.float32)).astype(jnp.bfloat16)
    return hi, mid, lo


def onehot_dot(onehot, x):
    return sum(jnp.dot(onehot, part, preferred_element_type=jnp.float32) for part in split3(x))


def kernel(
    footprints,
    tile_home,
    level_set,
    adjoint_source,
    primal_fields,
    grad_ref,
    peak_ref,
    src_in,
    prim_in,
    gathered,
    request,
    picked,
    returned,
    source,
    diff21,
    diff10,
    conduct,
    inverse,
    slope,
    va,
    vb,
    adjoint_two,
    outgoing,
    arrived,
    partial,
    owned,
    peaks,
    peaks2,
    local_sem,
    ag_send,
    ag_recv,
    rq_send,
    rq_recv,
    pk_send,
    pk_recv,
    og_send,
    og_recv,
    rs_send,
    rs_recv,
    fin_send,
    fin_recv,
    mp_send,
    mp_recv,
    mc_send,
    mc_recv,
):
    snd = lax.axis_index("snd")
    tile = lax.axis_index("tile")
    x, y = tile // 4, tile % 4
    z, core = snd // 2, snd % 2

    plane = []
    for i in range(1, 16):
        dx, dy = i // 4, i % 4
        plane.append((i, ((x + dx) % 4) * 4 + (y + dy) % 4))
    column = []
    for i in range(1, 8):
        dz, dc = i // 2, i % 2
        column.append((i, ((z + dz) % 4) * 2 + (core + dc) % 2))

    barrier = pltpu.get_barrier_semaphore()
    for _, to in plane:
        pl.semaphore_signal(barrier, inc=1, device_id=(snd, to), device_id_type=MESH)
    for _, to in column:
        pl.semaphore_signal(barrier, inc=1, device_id=(to, tile), device_id_type=MESH)

    own = []
    for p in range(PIECES):
        start = pl.multiple_of(snd * SLAB + p * PCELLS, PCELLS)
        own.append(
            pltpu.make_async_copy(
                level_set.at[:, pl.ds(start, PCELLS)], gathered.at[p, tile], local_sem.at[p]
            )
        )
        own[-1].start()
    load_src = pltpu.make_async_copy(adjoint_source, src_in, local_sem.at[PIECES])
    load_prim = pltpu.make_async_copy(primal_fields, prim_in, local_sem.at[PIECES + 1])
    load_src.start()
    load_prim.start()

    sends = []

    def start(src, dst, send_sem, recv_sem, to):
        copy = pltpu.make_async_remote_copy(src, dst, send_sem, recv_sem, to, MESH)
        copy.start()
        sends.append(copy)
        return copy

    wanted_rows = lax.broadcasted_iota(jnp.int32, (ENTRIES, TILES), 0)
    stored_rows = lax.broadcasted_iota(jnp.int32, (ENTRIES, TILES), 1)
    wanted = jnp.zeros((ENTRIES, TILES), jnp.int32)
    for j in range(ENTRIES):
        wanted = jnp.where(wanted_rows == j, tile_home[footprints[0, j]], wanted)
    mine = pl.ds(pl.multiple_of(snd * ENTRIES, ENTRIES), ENTRIES)
    request[mine, :] = jnp.where(wanted == stored_rows, 1.0, 0.0)

    for copy in own:
        copy.wait()
    pl.semaphore_wait(barrier, 22)

    ag, rq = [], []
    for p in range(PIECES):
        block = gathered.at[p, tile]
        ag.append([start(block, block, ag_send.at[p, i], ag_recv.at[p, i], (snd, to)) for i, to in plane])
        if p == 0:
            for i, to in column:
                rows = request.at[mine]
                rq.append(start(rows, rows, rq_send.at[i], rq_recv.at[i], (to, tile)))

    lane = lax.broadcasted_iota(jnp.int32, (DEPTH, 128), 1)
    left = lane < 64

    def halves(top, bottom):
        return (
            jnp.where(left, top, pltpu.roll(bottom, 64, 1)),
            jnp.where(left, pltpu.roll(top, 64, 1), bottom),
        )

    load_src.wait()
    load_prim.wait()

    def lay_out(rp, carry):
        low = pl.ds(pl.multiple_of(rp * 128, 128), 128)
        high = pl.ds(pl.multiple_of(rp * 128 + 2048, 128), 128)
        even, odd = halves(
            src_in[0, :, low].astype(jnp.float32), src_in[0, :, high].astype(jnp.float32)
        )
        source[2 * rp] = even
        source[2 * rp + 1] = odd
        fields = [
            [prim_in[0, k, :, part].astype(jnp.float32) for part in (low, high)] for k in range(3)
        ]
        even, odd = halves(fields[2][0] - fields[1][0], fields[2][1] - fields[1][1])
        diff21[2 * rp] = even
        diff21[2 * rp + 1] = odd
        even, odd = halves(fields[1][0] - fields[0][0], fields[1][1] - fields[0][1])
        diff10[2 * rp] = even
        diff10[2 * rp + 1] = odd
        return carry

    lax.fori_loop(0, 16, lay_out, 0, unroll=4)

    zeros8 = jnp.zeros((34, 8, 128), jnp.float32)
    for buf in (va, vb):
        buf[:, 0:8, :] = zeros8
        buf[:, 56:64, :] = zeros8

    lane_in = lax.broadcasted_iota(jnp.int32, (128, 128), 0)
    lane_out = lax.broadcasted_iota(jnp.int32, (128, 128), 1)
    apart = lane_in - lane_out
    beside = ((apart == 1) | (apart == -1)) & (lane_in // 64 == lane_out // 64)
    beside = jnp.where(beside, 1.0, 0.0).astype(jnp.bfloat16)
    beside = jnp.concatenate([beside, beside], axis=0)

    for copy in rq:
        copy.wait_recv()
    onehot = request[...]
    pick = onehot.astype(jnp.bfloat16)
    place = onehot.T.astype(jnp.bfloat16)
    pk = []
    for p in range(PIECES):
        for copy in ag[p]:
            copy.wait_recv()
        for c in range(PCHUNKS):
            cells = gathered[p, :, :, c * 128 : (c + 1) * 128].reshape(TILES, 128)
            picked[p, :, c * ENTRIES : (c + 1) * ENTRIES, :] = onehot_dot(pick, cells).reshape(
                NSND, ENTRIES, 128
            )
        rows = pl.ds(pl.multiple_of(snd * SROWS + p * PROWS, PROWS), PROWS)
        for i, to in column:
            pk.append(
                start(picked.at[p, to], returned.at[rows], pk_send.at[p, i], pk_recv.at[p, i], (to, tile))
            )
        returned[rows, :] = picked[p, snd]
    for copy in pk:
        copy.wait_recv()

    lane8 = lax.broadcasted_iota(jnp.int32, (8, 128), 1)

    def block_rows(step, g):
        db, rest = step // 4, step % 4
        th, b1 = rest // 2, rest % 2
        entry = (2 * (g // 4) + b1) * 4 + g % 4
        first = (db * 16 + th) * ENTRIES + entry
        return pl.ds(first, 8, stride=2 * ENTRIES), pl.multiple_of(db * 8, 8), b1 * 16 + th * 8

    def enter(step, carry):
        blocks = []
        for g in range(8):
            rows, depth, row = block_rows(step, g)
            blocks.append(returned[rows, :])
        for q, phi in enumerate(exchange_groups(blocks, lane8)):
            smooth = jnp.tanh(phi / front_width)
            cond = jnp.exp(log_low + 0.5 * log_span * (1.0 + smooth))
            at = pl.ds(depth, 8)
            inv = 1.0 / (6.0 + cond)
            conduct[row + q, at, :] = cond
            inverse[row + q, at, :] = inv
            slope[row + q, at, :] = (
                cond * (0.5 * log_span / front_width) * (1.0 - smooth * smooth)
            )
            va[row + q + 1, pl.ds(depth + 8, 8), :] = source[row + q, at, :] * inv
        return carry

    lax.fori_loop(0, 24, enter, 0, unroll=8)

    def sweep(now, keep):
        now[0, 8:56, :] = jnp.where(left, 0.0, pltpu.roll(now[32, 8:56, :], 64, 1))
        now[33, 8:56, :] = jnp.where(left, pltpu.roll(now[1, 8:56, :], 64, 1), 0.0)
        v = now[1:33, 8:56, :].reshape(32 * DEPTH, 128)
        hi = v.astype(jnp.bfloat16)
        lo = (v - hi.astype(jnp.float32)).astype(jnp.bfloat16)
        columns = jnp.dot(
            jnp.concatenate([hi, lo], axis=1), beside, preferred_element_type=jnp.float32
        ).reshape(32, DEPTH, 128)
        for row in range(32):
            total = now[row + 1, 7:55, :] + now[row + 1, 9:57, :]
            total = total + (now[row, 8:56, :] + now[row + 2, 8:56, :])
            total = total + columns[row]
            keep(row, (source[row] + total) * inverse[row])

    def solve(now, later, last):
        def into(buf):
            def keep(row, value):
                buf[row + 1, 8:56, :] = value

            return keep

        def pair(_, carry):
            sweep(now, into(later))
            sweep(later, into(now))
            return carry

        lax.fori_loop(0, (JACOBI - 2) // 2, pair, 0)
        sweep(now, last)

    def between(row, value):
        adjoint_two[row] = value
        rhs = conduct[row] * value
        source[row] = rhs
        vb[row + 1, 8:56, :] = rhs * inverse[row]

    def gradient(row, value):
        va[row + 1, 8:56, :] = -slope[row] * (
            adjoint_two[row] * diff21[row] + value * diff10[row]
        )

    solve(va, vb, between)
    solve(vb, va, gradient)

    def leave(step, carry):
        _, depth, row = block_rows(step, 0)
        blocks = [va[row + q + 1, pl.ds(depth + 8, 8), :] for q in range(8)]
        for g, block in enumerate(exchange_groups(blocks, lane8)):
            rows, _, _ = block_rows(step, g)
            outgoing[rows, :] = block
        return carry

    lax.fori_loop(0, 24, leave, 0, unroll=8)

    og = []
    for p in range(PIECES):
        og.append([])
        for i, to in column:
            rows = pl.ds(pl.multiple_of(to * SROWS + p * PROWS, PROWS), PROWS)
            og[p].append(
                start(outgoing.at[rows], arrived.at[p, snd], og_send.at[p, i], og_recv.at[p, i], (to, tile))
            )
        rows = pl.ds(pl.multiple_of(snd * SROWS + p * PROWS, PROWS), PROWS)
        arrived[p, snd] = outgoing[rows, :]

    rs = []
    for p in range(PIECES):
        for copy in og[p]:
            copy.wait_recv()
        for c in range(PCHUNKS):
            cells = arrived[p, :, c * ENTRIES : (c + 1) * ENTRIES, :].reshape(TILES, 128)
            partial[p, :, :, c * 128 : (c + 1) * 128] = onehot_dot(place, cells).reshape(
                NTILE, TDEV, 128
            )
        rs.append(
            [
                start(partial.at[p, to], owned.at[p, tile], rs_send.at[p, i], rs_recv.at[p, i], (snd, to))
                for i, to in plane
            ]
        )
        owned[p, tile] = partial[p, tile]

    fin = []
    top = jnp.zeros((TDEV, 128), jnp.float32)
    for p in range(PIECES):
        for copy in rs[p]:
            copy.wait_recv()
        slab = owned[p, 0]
        for i in range(1, NTILE):
            slab = slab + owned[p, i]
        cells = pl.ds(pl.multiple_of(snd * SLAB + p * PCELLS, PCELLS), PCELLS)
        grad_ref[:, cells] = slab
        size = jnp.abs(slab)
        for c in range(PCHUNKS):
            top = jnp.maximum(top, size[:, c * 128 : (c + 1) * 128])
        if p == PIECES - 1:
            peaks[tile] = top
            mp = [
                start(peaks.at[tile], peaks.at[tile], mp_send.at[i], mp_recv.at[i], (snd, to))
                for i, to in plane
            ]
        block = grad_ref.at[:, cells]
        for i, to in column:
            fin.append(start(block, block, fin_send.at[p, i], fin_recv.at[p, i], (to, tile)))

    for copy in mp:
        copy.wait_recv()
    top = peaks[0]
    for i in range(1, NTILE):
        top = jnp.maximum(top, peaks[i])
    peaks2[snd] = top
    mc = [
        start(peaks2.at[snd], peaks2.at[snd], mc_send.at[i], mc_recv.at[i], (to, tile))
        for i, to in column
    ]
    for copy in mc:
        copy.wait_recv()
    top = peaks2[0]
    for i in range(1, NSND):
        top = jnp.maximum(top, peaks2[i])
    peak_ref[...] = top
    for copy in fin:
        copy.wait_recv()
    for copy in sends:
        copy.wait_send()


def finish(grad, peak, level_set, grad_out, next_out, grad_in, peak_in, level_in, blank, sem):
    rest = level_set.shape[1] - TOP
    head, tail = pl.ds(0, TOP), pl.ds(TOP, rest)

    def copy(i, src, dst):
        c = pltpu.make_async_copy(src, dst, sem.at[i])
        c.start()
        return c

    reads = [
        copy(0, level_set.at[:, tail], level_in.at[:, tail]),
        copy(1, peak, peak_in),
        copy(2, grad, grad_in),
        copy(3, level_set.at[:, head], level_in.at[:, head]),
    ]
    blank[...] = jnp.zeros((TDEV, rest), jnp.float32)
    writes = [copy(4, blank, grad_out.at[:, tail])]
    reads[0].wait()
    writes.append(copy(5, level_in.at[:, tail], next_out.at[:, tail]))
    for c in reads[1:3]:
        c.wait()
    writes.append(copy(6, grad_in, grad_out.at[:, head]))
    scale = step_size / (jnp.max(peak_in[...]) + 1e-6)
    reads[3].wait()
    level_in[:, head] = level_in[:, head] - scale * grad_in[...]
    writes.append(copy(7, level_in.at[:, head], next_out.at[:, head]))
    for c in writes:
        c.wait()


def shards(level_set, tile_home, footprints, adjoint_source, primal_fields):
    f32 = jnp.float32
    smem = pl.BlockSpec(memory_space=pltpu.SMEM)
    anywhere = pl.BlockSpec(memory_space=pltpu.HBM)
    vmem = pl.BlockSpec(memory_space=pltpu.VMEM)
    field = pltpu.VMEM((32, DEPTH, 128), f32)
    padded = pltpu.VMEM((34, DEPTH + 16, 128), f32)
    dma = pltpu.SemaphoreType.DMA
    grad, peak = pl.pallas_call(
        kernel,
        out_shape=(
            jax.ShapeDtypeStruct((TDEV, TOP), f32),
            jax.ShapeDtypeStruct((8, 128), f32),
        ),
        in_specs=[smem, smem, anywhere, anywhere, anywhere],
        out_specs=(vmem, vmem),
        scratch_shapes=[
            pltpu.VMEM(adjoint_source.shape, jnp.bfloat16),
            pltpu.VMEM(primal_fields.shape, jnp.bfloat16),
            pltpu.VMEM((PIECES, NTILE, TDEV, PCELLS), f32),
            pltpu.VMEM((NSND * ENTRIES, TILES), f32),
            pltpu.VMEM((PIECES, NSND, PROWS, 128), f32),
            pltpu.VMEM((NSND * SROWS, 128), f32),
            field,
            field,
            field,
            field,
            field,
            field,
            padded,
            padded,
            field,
            pltpu.VMEM((NSND * SROWS, 128), f32),
            pltpu.VMEM((PIECES, NSND, PROWS, 128), f32),
            pltpu.VMEM((PIECES, NTILE, TDEV, PCELLS), f32),
            pltpu.VMEM((PIECES, NTILE, TDEV, PCELLS), f32),
            pltpu.VMEM((NTILE, 8, 128), f32),
            pltpu.VMEM((NSND, 8, 128), f32),
            dma((PIECES + 2,)),
            dma((PIECES, NTILE)),
            dma((PIECES, NTILE)),
            dma((NSND,)),
            dma((NSND,)),
            dma((PIECES, NSND)),
            dma((PIECES, NSND)),
            dma((PIECES, NSND)),
            dma((PIECES, NSND)),
            dma((PIECES, NTILE)),
            dma((PIECES, NTILE)),
            dma((PIECES, NSND)),
            dma((PIECES, NSND)),
            dma((NTILE,)),
            dma((NTILE,)),
            dma((NSND,)),
            dma((NSND,)),
        ],
        compiler_params=pltpu.CompilerParams(
            collective_id=0, has_side_effects=True, vmem_limit_bytes=VMEM_LIMIT
        ),
    )(footprints, tile_home, level_set, adjoint_source, primal_fields)
    out = jax.ShapeDtypeStruct(level_set.shape, f32)
    return pl.pallas_call(
        finish,
        out_shape=(out, out),
        in_specs=[anywhere, anywhere, anywhere],
        out_specs=(anywhere, anywhere),
        scratch_shapes=[
            pltpu.VMEM((TDEV, TOP), f32),
            pltpu.VMEM((8, 128), f32),
            pltpu.VMEM(level_set.shape, f32),
            pltpu.VMEM((TDEV, level_set.shape[1] - TOP), f32),
            dma((8,)),
        ],
        compiler_params=pltpu.CompilerParams(vmem_limit_bytes=VMEM_LIMIT),
    )(grad, peak, level_set)


def solution(mesh):
    return jax.shard_map(
        shards,
        mesh=mesh,
        in_specs=(
            P("tile", None),
            P(),
            P(("snd", "tile"), None),
            P(("snd", "tile"), None, None),
            P(("snd", "tile"), None, None, None),
        ),
        out_specs=(P("tile", None), P("tile", None)),
        check_vma=False,
    )
```

time: 124 us -> 69.1 us (0.56)
  Pallas kernels: 118 us -> 67.2 us
  local copies, waits for them, and re-layouts: 4.77 us -> 0 us
    pallas_call x1, Pallas kernels: 116 us -> 64.8 us  [shards(): pl.pallas_call(kernel, out_shape=(jax.ShapeDtypeStruct((TDEV, TOP), f32),...]
    unnamed x12 -> x0, local copies, waits for them, and re-layouts: 4.77 us -> none
where the time goes in v2:
time: 69.1 us; the launch traced here: 67.9 us
  Pallas kernels  67.2 us (97%)
    pallas_call x1, Pallas kernels, shards(): pl.pallas_call(kernel, out_shape=(jax.ShapeDtypeStruct((TDEV, TOP), f32),...  64.8 us
    pallas_call x1, Pallas kernels, shards(): pl.pallas_call(finish, out_shape=(out, out), in_specs=[anywhere, anywhere...  2.42 us

profile of v2, /device:TPU:0, one launch (start us, length us, event | category | flops | bytes accessed | tf_op | source)
XLA Modules:
  0.0 67.9 jit_solution(8511370877478062865)
XLA Ops:
  0.6 64.8 %shard_map.68 = (f32[8,12288]{1,0:T(8,128)}, f32[8,128]{1,0:T(8,128)}) custom-call(s32[1,16]{1,0:T(1,128)} %footprints.1, s32[128]{0:T(128)} %tile_home.1, f32[8,30720]{1,0:T(8,128)} %level_set.3, bf16[1,48,4096]{2,1,0:T(8,128)(2,1)} %adjoint_source.1, bf16[1,3,48,4096]{3,2,1,0:T(8,128)(2,1)} %primal_fields.1), custom_call_target="tpu_custom_call" | custom-call | tf_op jit(solution)/shard_map/pallas_call | solution.py:431
  65.5 2.4 %shard_map.69 = (f32[8,30720]{1,0:T(8,128)}, f32[8,30720]{1,0:T(8,128)}) custom-call(f32[8,12288]{1,0:T(8,128)} %get-tuple-element.4.grad, f32[8,128]{1,0:T(8,128)} %get-tuple-element.5.peak, f32[8,30720]{1,0:T(8,128)} %level_set.3), custom_call_target="tpu_custom_call" | custom-call | tf_op jit(solution)/shard_map/pallas_call | solution.py:484

commit v3 on v2

--- a/solution.py
+++ b/solution.py
@@ -22,10 +22,14 @@
 SLAB = TOP // NSND
 CHUNKS = SLAB // 128
 SROWS = CHUNKS * ENTRIES
-PIECES = 3
-PCHUNKS = CHUNKS // PIECES
-PCELLS = SLAB // PIECES
-PROWS = SROWS // PIECES
+DEPTHS = (16, 16, 16)
+PIECES = len(DEPTHS)
+FIRST = [sum(DEPTHS[:p]) for p in range(PIECES)]
+PCHUNKS = [d // 4 for d in DEPTHS]
+MOST = max(PCHUNKS)
+
+PLANE = ((2, 2), (1, 2), (3, 2), (2, 1), (2, 3), (1, 1), (3, 3), (1, 3), (3, 1), (0, 2), (2, 0), (0, 1), (0, 3), (1, 0), (3, 0))
+COLUMN = ((2, 1), (2, 0), (1, 1), (3, 1), (1, 0), (3, 0), (0, 1))
 
 VMEM_LIMIT = 60 * 1024 * 1024
 
@@ -56,13 +60,31 @@
     return sum(jnp.dot(onehot, part, preferred_element_type=jnp.float32) for part in split3(x))
 
 
+def within(p):
+    return pl.ds(0, PCHUNKS[p] * 128)
+
+
+def piece_cells(p, k):
+    size = PCHUNKS[p] * 128
+    return pl.ds(pl.multiple_of(FIRST[p] * TX * TX + k * size, 128), size)
+
+
+def piece_rows(p, k):
+    size = PCHUNKS[p] * ENTRIES
+    return pl.ds(pl.multiple_of(FIRST[p] * 2 * ENTRIES + k * size, ENTRIES), size)
+
+
+def piece_steps(p):
+    return FIRST[p] // 2, (FIRST[p] + DEPTHS[p]) // 2
+
+
 def kernel(
     footprints,
     tile_home,
     level_set,
     adjoint_source,
     primal_fields,
-    grad_ref,
+    grad_out,
     peak_ref,
     src_in,
     prim_in,
@@ -85,6 +107,7 @@
     owned,
     peaks,
     peaks2,
+    grad_ref,
     local_sem,
     ag_send,
     ag_recv,
@@ -109,13 +132,11 @@
     z, core = snd // 2, snd % 2
 
     plane = []
-    for i in range(1, 16):
-        dx, dy = i // 4, i % 4
-        plane.append((i, ((x + dx) % 4) * 4 + (y + dy) % 4))
+    for dx, dy in PLANE:
+        plane.append((4 * dx + dy, ((x + dx) % 4) * 4 + (y + dy) % 4))
     column = []
-    for i in range(1, 8):
-        dz, dc = i // 2, i % 2
-        column.append((i, ((z + dz) % 4) * 2 + (core + dc) % 2))
+    for dz, dc in COLUMN:
+        column.append((2 * dz + dc, ((z + dz) % 4) * 2 + (core + dc) % 2))
 
     barrier = pltpu.get_barrier_semaphore()
     for _, to in plane:
@@ -125,10 +146,10 @@
 
     own = []
     for p in range(PIECES):
-        start = pl.multiple_of(snd * SLAB + p * PCELLS, PCELLS)
+        cells = piece_cells(p, snd)
         own.append(
             pltpu.make_async_copy(
-                level_set.at[:, pl.ds(start, PCELLS)], gathered.at[p, tile], local_sem.at[p]
+                level_set.at[:, cells], gathered.at[p, tile, :, within(p)], local_sem.at[p]
             )
         )
         own[-1].start()
@@ -145,6 +166,11 @@
         sends.append(copy)
         return copy
 
+    def drain(count):
+        for copy in sends[: len(sends) - count]:
+            copy.wait_send()
+        del sends[: len(sends) - count]
+
     wanted_rows = lax.broadcasted_iota(jnp.int32, (ENTRIES, TILES), 0)
     stored_rows = lax.broadcasted_iota(jnp.int32, (ENTRIES, TILES), 1)
     wanted = jnp.zeros((ENTRIES, TILES), jnp.int32)
@@ -159,7 +185,7 @@
 
     ag, rq = [], []
     for p in range(PIECES):
-        block = gathered.at[p, tile]
+        block = gathered.at[p, tile, :, within(p)]
         ag.append([start(block, block, ag_send.at[p, i], ag_recv.at[p, i], (snd, to)) for i, to in plane])
         if p == 0:
             for i, to in column:
@@ -220,19 +246,21 @@
     for p in range(PIECES):
         for copy in ag[p]:
             copy.wait_recv()
-        for c in range(PCHUNKS):
+        for c in range(PCHUNKS[p]):
             cells = gathered[p, :, :, c * 128 : (c + 1) * 128].reshape(TILES, 128)
             picked[p, :, c * ENTRIES : (c + 1) * ENTRIES, :] = onehot_dot(pick, cells).reshape(
                 NSND, ENTRIES, 128
             )
-        rows = pl.ds(pl.multiple_of(snd * SROWS + p * PROWS, PROWS), PROWS)
-        for i, to in column:
-            pk.append(
-                start(picked.at[p, to], returned.at[rows], pk_send.at[p, i], pk_recv.at[p, i], (to, tile))
-            )
-        returned[rows, :] = picked[p, snd]
-    for copy in pk:
-        copy.wait_recv()
+        rows = piece_rows(p, snd)
+        pk.append(
+            [
+                start(picked.at[p, to, 0 : PCHUNKS[p] * ENTRIES], returned.at[rows], pk_send.at[p, i], pk_recv.at[p, i], (to, tile))
+                for i, to in column
+            ]
+        )
+        returned[rows, :] = picked[p, snd, 0 : PCHUNKS[p] * ENTRIES]
+
+    drain(PIECES * 7)
 
     lane8 = lax.broadcasted_iota(jnp.int32, (8, 128), 1)
 
@@ -261,7 +289,10 @@
             va[row + q + 1, pl.ds(depth + 8, 8), :] = source[row + q, at, :] * inv
         return carry
 
-    lax.fori_loop(0, 24, enter, 0, unroll=8)
+    for p in range(PIECES):
+        for copy in pk[p]:
+            copy.wait_recv()
+        lax.fori_loop(*piece_steps(p), enter, 0, unroll=min(8, DEPTHS[p] // 2))
 
     def sweep(now, keep):
         now[0, 8:56, :] = jnp.where(left, 0.0, pltpu.roll(now[32, 8:56, :], 64, 1))
@@ -315,48 +346,51 @@
             outgoing[rows, :] = block
         return carry
 
-    lax.fori_loop(0, 24, leave, 0, unroll=8)
-
     og = []
     for p in range(PIECES):
+        lax.fori_loop(*piece_steps(p), leave, 0, unroll=min(8, DEPTHS[p] // 2))
         og.append([])
         for i, to in column:
-            rows = pl.ds(pl.multiple_of(to * SROWS + p * PROWS, PROWS), PROWS)
+            rows = piece_rows(p, to)
             og[p].append(
-                start(outgoing.at[rows], arrived.at[p, snd], og_send.at[p, i], og_recv.at[p, i], (to, tile))
+                start(outgoing.at[rows], arrived.at[p, snd, 0 : PCHUNKS[p] * ENTRIES], og_send.at[p, i], og_recv.at[p, i], (to, tile))
             )
-        rows = pl.ds(pl.multiple_of(snd * SROWS + p * PROWS, PROWS), PROWS)
-        arrived[p, snd] = outgoing[rows, :]
+        rows = piece_rows(p, snd)
+        arrived[p, snd, 0 : PCHUNKS[p] * ENTRIES] = outgoing[rows, :]
+
+    drain(PIECES * 7)
 
     rs = []
     for p in range(PIECES):
         for copy in og[p]:
             copy.wait_recv()
-        for c in range(PCHUNKS):
+        for c in range(PCHUNKS[p]):
             cells = arrived[p, :, c * ENTRIES : (c + 1) * ENTRIES, :].reshape(TILES, 128)
             partial[p, :, :, c * 128 : (c + 1) * 128] = onehot_dot(place, cells).reshape(
                 NTILE, TDEV, 128
             )
         rs.append(
             [
-                start(partial.at[p, to], owned.at[p, tile], rs_send.at[p, i], rs_recv.at[p, i], (snd, to))
+                start(partial.at[p, to, :, within(p)], owned.at[p, tile, :, within(p)], rs_send.at[p, i], rs_recv.at[p, i], (snd, to))
                 for i, to in plane
             ]
         )
-        owned[p, tile] = partial[p, tile]
+        owned[p, tile, :, within(p)] = partial[p, tile, :, within(p)]
+
+    drain(PIECES * 15)
 
     fin = []
     top = jnp.zeros((TDEV, 128), jnp.float32)
     for p in range(PIECES):
         for copy in rs[p]:
             copy.wait_recv()
-        slab = owned[p, 0]
+        slab = owned[p, 0, :, within(p)]
         for i in range(1, NTILE):
-            slab = slab + owned[p, i]
-        cells = pl.ds(pl.multiple_of(snd * SLAB + p * PCELLS, PCELLS), PCELLS)
+            slab = slab + owned[p, i, :, within(p)]
+        cells = piece_cells(p, snd)
         grad_ref[:, cells] = slab
         size = jnp.abs(slab)
-        for c in range(PCHUNKS):
+        for c in range(PCHUNKS[p]):
             top = jnp.maximum(top, size[:, c * 128 : (c + 1) * 128])
         if p == PIECES - 1:
             peaks[tile] = top
@@ -368,6 +402,8 @@
         for i, to in column:
             fin.append(start(block, block, fin_send.at[p, i], fin_recv.at[p, i], (to, tile)))
 
+    drain(15 + 7)
+
     for copy in mp:
         copy.wait_recv()
     top = peaks[0]
@@ -378,16 +414,19 @@
         start(peaks2.at[snd], peaks2.at[snd], mc_send.at[i], mc_recv.at[i], (to, tile))
         for i, to in column
     ]
+    drain(7)
+    for copy in fin:
+        copy.wait_recv()
+    store = pltpu.make_async_copy(grad_ref, grad_out, local_sem.at[0])
+    store.start()
     for copy in mc:
         copy.wait_recv()
     top = peaks2[0]
     for i in range(1, NSND):
         top = jnp.maximum(top, peaks2[i])
     peak_ref[...] = top
-    for copy in fin:
-        copy.wait_recv()
-    for copy in sends:
-        copy.wait_send()
+    drain(0)
+    store.wait()
 
 
 def finish(grad, peak, level_set, grad_out, next_out, grad_in, peak_in, level_in, blank, sem):
@@ -435,13 +474,13 @@
             jax.ShapeDtypeStruct((8, 128), f32),
         ),
         in_specs=[smem, smem, anywhere, anywhere, anywhere],
-        out_specs=(vmem, vmem),
+        out_specs=(anywhere, vmem),
         scratch_shapes=[
             pltpu.VMEM(adjoint_source.shape, jnp.bfloat16),
             pltpu.VMEM(primal_fields.shape, jnp.bfloat16),
-            pltpu.VMEM((PIECES, NTILE, TDEV, PCELLS), f32),
+            pltpu.VMEM((PIECES, NTILE, TDEV, MOST * 128), f32),
             pltpu.VMEM((NSND * ENTRIES, TILES), f32),
-            pltpu.VMEM((PIECES, NSND, PROWS, 128), f32),
+            pltpu.VMEM((PIECES, NSND, MOST * ENTRIES, 128), f32),
             pltpu.VMEM((NSND * SROWS, 128), f32),
             field,
             field,
@@ -453,11 +492,12 @@
             padded,
             field,
             pltpu.VMEM((NSND * SROWS, 128), f32),
-            pltpu.VMEM((PIECES, NSND, PROWS, 128), f32),
-            pltpu.VMEM((PIECES, NTILE, TDEV, PCELLS), f32),
-            pltpu.VMEM((PIECES, NTILE, TDEV, PCELLS), f32),
+            pltpu.VMEM((PIECES, NSND, MOST * ENTRIES, 128), f32),
+            pltpu.VMEM((PIECES, NTILE, TDEV, MOST * 128), f32),
+            pltpu.VMEM((PIECES, NTILE, TDEV, MOST * 128), f32),
             pltpu.VMEM((NTILE, 8, 128), f32),
             pltpu.VMEM((NSND, 8, 128), f32),
+            pltpu.VMEM((TDEV, TOP), f32),
             dma((PIECES + 2,)),
             dma((PIECES, NTILE)),
             dma((PIECES, NTILE)),

time: 69.1 us -> 64 us (0.926)
  Pallas kernels: 67.2 us -> 62.3 us
    pallas_call x1, Pallas kernels: 64.8 us -> 59.9 us  [shards(): pl.pallas_call(kernel, out_shape=(jax.ShapeDtypeStruct((TDEV, TOP), f32),...]
where the time goes in v3:
time: 64 us; the launch traced here: 63 us
  Pallas kernels  62.3 us (97%)
  between operations  0.64 us (1%)
    pallas_call x1, Pallas kernels, shards(): pl.pallas_call(kernel, out_shape=(jax.ShapeDtypeStruct((TDEV, TOP), f32),...  59.9 us
    pallas_call x1, Pallas kernels, shards(): pl.pallas_call(finish, out_shape=(out, out), in_specs=[anywhere, anywhere...  2.42 us

profile of v3, /device:TPU:0, one launch (start us, length us, event | category | flops | bytes accessed | tf_op | source)
XLA Modules:
  0.0 63.0 jit_solution(5045914773309945362)
XLA Ops:
  0.6 59.9 %shard_map.68 = (f32[8,12288]{1,0:T(8,128)}, f32[8,128]{1,0:T(8,128)}) custom-call(s32[1,16]{1,0:T(1,128)} %footprints.1, s32[128]{0:T(128)} %tile_home.1, f32[8,30720]{1,0:T(8,128)} %level_set.3, bf16[1,48,4096]{2,1,0:T(8,128)(2,1)} %adjoint_source.1, bf16[1,3,48,4096]{3,2,1,0:T(8,128)(2,1)} %primal_fields.1), custom_call_target="tpu_custom_call" | custom-call | tf_op jit(solution)/shard_map/pallas_call | solution.py:470
  60.5 2.4 %shard_map.69 = (f32[8,30720]{1,0:T(8,128)}, f32[8,30720]{1,0:T(8,128)}) custom-call(f32[8,12288]{1,0:T(8,128)} %get-tuple-element.4.grad, f32[8,128]{1,0:T(8,128)} %get-tuple-element.5.peak, f32[8,30720]{1,0:T(8,128)} %level_set.3), custom_call_target="tpu_custom_call" | custom-call | tf_op jit(solution)/shard_map/pallas_call | solution.py:524

commit v4 on v3

--- a/solution.py
+++ b/solution.py
@@ -22,7 +22,7 @@
 SLAB = TOP // NSND
 CHUNKS = SLAB // 128
 SROWS = CHUNKS * ENTRIES
-DEPTHS = (16, 16, 16)
+DEPTHS = (8, 8, 8, 8, 8, 8)
 PIECES = len(DEPTHS)
 FIRST = [sum(DEPTHS[:p]) for p in range(PIECES)]
 PCHUNKS = [d // 4 for d in DEPTHS]
@@ -72,6 +72,10 @@
 def piece_rows(p, k):
     size = PCHUNKS[p] * ENTRIES
     return pl.ds(pl.multiple_of(FIRST[p] * 2 * ENTRIES + k * size, ENTRIES), size)
+
+
+def piece_seven(p):
+    return pl.ds(0, 7 * PCHUNKS[p] * ENTRIES)
 
 
 def piece_steps(p):
@@ -133,15 +137,15 @@
 
     plane = []
     for dx, dy in PLANE:
-        plane.append((4 * dx + dy, ((x + dx) % 4) * 4 + (y + dy) % 4))
+        plane.append((x + dx) % 4 * 4 + (y + dy) % 4)
     column = []
     for dz, dc in COLUMN:
-        column.append((2 * dz + dc, ((z + dz) % 4) * 2 + (core + dc) % 2))
+        column.append((z + dz) % 4 * 2 + (core + dc) % 2)
 
     barrier = pltpu.get_barrier_semaphore()
-    for _, to in plane:
+    for to in plane:
         pl.semaphore_signal(barrier, inc=1, device_id=(snd, to), device_id_type=MESH)
-    for _, to in column:
+    for to in column:
         pl.semaphore_signal(barrier, inc=1, device_id=(to, tile), device_id_type=MESH)
 
     own = []
@@ -160,16 +164,22 @@
 
     sends = []
 
-    def start(src, dst, send_sem, recv_sem, to):
-        copy = pltpu.make_async_remote_copy(src, dst, send_sem, recv_sem, to, MESH)
-        copy.start()
-        sends.append(copy)
-        return copy
-
-    def drain(count):
-        for copy in sends[: len(sends) - count]:
-            copy.wait_send()
-        del sends[: len(sends) - count]
+    def send_all(parts, send_sem, recv_sem, whole):
+        for src, dst, to in parts:
+            pltpu.make_async_remote_copy(src, dst, send_sem, recv_sem, to, MESH).start()
+        sends.append((whole, send_sem))
+        return whole, recv_sem
+
+    def wait_all(pair):
+        whole, sem = pair
+        pltpu.make_async_copy(whole, whole, sem).wait()
+
+    waited = [0]
+
+    def drain(mark):
+        for pair in sends[waited[0] : mark]:
+            wait_all(pair)
+        waited[0] = mark
 
     wanted_rows = lax.broadcasted_iota(jnp.int32, (ENTRIES, TILES), 0)
     stored_rows = lax.broadcasted_iota(jnp.int32, (ENTRIES, TILES), 1)
@@ -183,14 +193,25 @@
         copy.wait()
     pl.semaphore_wait(barrier, 22)
 
-    ag, rq = [], []
+    ag = []
     for p in range(PIECES):
         block = gathered.at[p, tile, :, within(p)]
-        ag.append([start(block, block, ag_send.at[p, i], ag_recv.at[p, i], (snd, to)) for i, to in plane])
+        ag.append(
+            send_all(
+                [(block, block, (snd, to)) for to in plane],
+                ag_send.at[p],
+                ag_recv.at[p],
+                gathered.at[p, 0:15, :, within(p)],
+            )
+        )
         if p == 0:
-            for i, to in column:
-                rows = request.at[mine]
-                rq.append(start(rows, rows, rq_send.at[i], rq_recv.at[i], (to, tile)))
+            rows = request.at[mine]
+            rq = send_all(
+                [(rows, rows, (to, tile)) for to in column],
+                rq_send.at[0],
+                rq_recv.at[0],
+                request.at[0 : 7 * ENTRIES],
+            )
 
     lane = lax.broadcasted_iota(jnp.int32, (DEPTH, 128), 1)
     left = lane < 64
@@ -237,30 +258,32 @@
     beside = jnp.where(beside, 1.0, 0.0).astype(jnp.bfloat16)
     beside = jnp.concatenate([beside, beside], axis=0)
 
-    for copy in rq:
-        copy.wait_recv()
+    wait_all(rq)
     onehot = request[...]
     pick = onehot.astype(jnp.bfloat16)
     place = onehot.T.astype(jnp.bfloat16)
+    gather_sends = len(sends)
     pk = []
     for p in range(PIECES):
-        for copy in ag[p]:
-            copy.wait_recv()
+        wait_all(ag[p])
         for c in range(PCHUNKS[p]):
             cells = gathered[p, :, :, c * 128 : (c + 1) * 128].reshape(TILES, 128)
             picked[p, :, c * ENTRIES : (c + 1) * ENTRIES, :] = onehot_dot(pick, cells).reshape(
                 NSND, ENTRIES, 128
             )
         rows = piece_rows(p, snd)
+        size = PCHUNKS[p] * ENTRIES
         pk.append(
-            [
-                start(picked.at[p, to, 0 : PCHUNKS[p] * ENTRIES], returned.at[rows], pk_send.at[p, i], pk_recv.at[p, i], (to, tile))
-                for i, to in column
-            ]
+            send_all(
+                [(picked.at[p, to, 0:size], returned.at[rows], (to, tile)) for to in column],
+                pk_send.at[p],
+                pk_recv.at[p],
+                returned.at[piece_seven(p)],
+            )
         )
         returned[rows, :] = picked[p, snd, 0 : PCHUNKS[p] * ENTRIES]
 
-    drain(PIECES * 7)
+    drain(gather_sends)
 
     lane8 = lax.broadcasted_iota(jnp.int32, (8, 128), 1)
 
@@ -290,8 +313,7 @@
         return carry
 
     for p in range(PIECES):
-        for copy in pk[p]:
-            copy.wait_recv()
+        wait_all(pk[p])
         lax.fori_loop(*piece_steps(p), enter, 0, unroll=min(8, DEPTHS[p] // 2))
 
     def sweep(now, keep):
@@ -346,44 +368,56 @@
             outgoing[rows, :] = block
         return carry
 
+    pick_sends = len(sends)
     og = []
     for p in range(PIECES):
         lax.fori_loop(*piece_steps(p), leave, 0, unroll=min(8, DEPTHS[p] // 2))
-        og.append([])
-        for i, to in column:
-            rows = piece_rows(p, to)
-            og[p].append(
-                start(outgoing.at[rows], arrived.at[p, snd, 0 : PCHUNKS[p] * ENTRIES], og_send.at[p, i], og_recv.at[p, i], (to, tile))
-            )
+        size = PCHUNKS[p] * ENTRIES
+        og.append(
+            send_all(
+                [
+                    (outgoing.at[piece_rows(p, to)], arrived.at[p, snd, 0:size], (to, tile))
+                    for to in column
+                ],
+                og_send.at[p],
+                og_recv.at[p],
+                arrived.at[p, 0:7, 0:size],
+            )
+        )
         rows = piece_rows(p, snd)
         arrived[p, snd, 0 : PCHUNKS[p] * ENTRIES] = outgoing[rows, :]
 
-    drain(PIECES * 7)
-
+    drain(pick_sends)
+
+    og_sends = len(sends)
     rs = []
     for p in range(PIECES):
-        for copy in og[p]:
-            copy.wait_recv()
+        wait_all(og[p])
         for c in range(PCHUNKS[p]):
             cells = arrived[p, :, c * ENTRIES : (c + 1) * ENTRIES, :].reshape(TILES, 128)
             partial[p, :, :, c * 128 : (c + 1) * 128] = onehot_dot(place, cells).reshape(
                 NTILE, TDEV, 128
             )
         rs.append(
-            [
-                start(partial.at[p, to, :, within(p)], owned.at[p, tile, :, within(p)], rs_send.at[p, i], rs_recv.at[p, i], (snd, to))
-                for i, to in plane
-            ]
+            send_all(
+                [
+                    (partial.at[p, to, :, within(p)], owned.at[p, tile, :, within(p)], (snd, to))
+                    for to in plane
+                ],
+                rs_send.at[p],
+                rs_recv.at[p],
+                owned.at[p, 0:15, :, within(p)],
+            )
         )
         owned[p, tile, :, within(p)] = partial[p, tile, :, within(p)]
 
-    drain(PIECES * 15)
-
+    drain(og_sends)
+
+    rs_sends = len(sends)
     fin = []
     top = jnp.zeros((TDEV, 128), jnp.float32)
     for p in range(PIECES):
-        for copy in rs[p]:
-            copy.wait_recv()
+        wait_all(rs[p])
         slab = owned[p, 0, :, within(p)]
         for i in range(1, NTILE):
             slab = slab + owned[p, i, :, within(p)]
@@ -393,39 +427,40 @@
         for c in range(PCHUNKS[p]):
             top = jnp.maximum(top, size[:, c * 128 : (c + 1) * 128])
         if p == PIECES - 1:
-            peaks[tile] = top
-            mp = [
-                start(peaks.at[tile], peaks.at[tile], mp_send.at[i], mp_recv.at[i], (snd, to))
-                for i, to in plane
-            ]
+            peaks[tile] = jnp.max(top, axis=0, keepdims=True)
+            peak = peaks.at[tile]
+            mp = send_all(
+                [(peak, peak, (snd, to)) for to in plane],
+                mp_send.at[0],
+                mp_recv.at[0],
+                peaks.at[0:15],
+            )
         block = grad_ref.at[:, cells]
-        for i, to in column:
-            fin.append(start(block, block, fin_send.at[p, i], fin_recv.at[p, i], (to, tile)))
-
-    drain(15 + 7)
-
-    for copy in mp:
-        copy.wait_recv()
-    top = peaks[0]
-    for i in range(1, NTILE):
-        top = jnp.maximum(top, peaks[i])
-    peaks2[snd] = top
-    mc = [
-        start(peaks2.at[snd], peaks2.at[snd], mc_send.at[i], mc_recv.at[i], (to, tile))
-        for i, to in column
-    ]
-    drain(7)
-    for copy in fin:
-        copy.wait_recv()
+        fin.append(
+            send_all(
+                [(block, block, (to, tile)) for to in column],
+                fin_send.at[p],
+                fin_recv.at[p],
+                grad_ref.at[:, pl.ds(0, 7 * PCHUNKS[p] * 128)],
+            )
+        )
+
+    drain(rs_sends)
+
+    wait_all(mp)
+    peaks2[snd] = jnp.max(peaks[...], axis=0)
+    peak = peaks2.at[snd]
+    mc = send_all(
+        [(peak, peak, (to, tile)) for to in column], mc_send.at[0], mc_recv.at[0], peaks2.at[0:7]
+    )
+    drain(len(sends) - 1)
+    for pair in fin:
+        wait_all(pair)
     store = pltpu.make_async_copy(grad_ref, grad_out, local_sem.at[0])
     store.start()
-    for copy in mc:
-        copy.wait_recv()
-    top = peaks2[0]
-    for i in range(1, NSND):
-        top = jnp.maximum(top, peaks2[i])
-    peak_ref[...] = top
-    drain(0)
+    wait_all(mc)
+    peak_ref[...] = jnp.broadcast_to(jnp.max(peaks2[...], axis=0), (8, 128))
+    drain(len(sends))
     store.wait()
 
 
@@ -495,26 +530,26 @@
             pltpu.VMEM((PIECES, NSND, MOST * ENTRIES, 128), f32),
             pltpu.VMEM((PIECES, NTILE, TDEV, MOST * 128), f32),
             pltpu.VMEM((PIECES, NTILE, TDEV, MOST * 128), f32),
-            pltpu.VMEM((NTILE, 8, 128), f32),
-            pltpu.VMEM((NSND, 8, 128), f32),
+            pltpu.VMEM((NTILE, 1, 128), f32),
+            pltpu.VMEM((NSND, 1, 128), f32),
             pltpu.VMEM((TDEV, TOP), f32),
             dma((PIECES + 2,)),
-            dma((PIECES, NTILE)),
-            dma((PIECES, NTILE)),
-            dma((NSND,)),
-            dma((NSND,)),
-            dma((PIECES, NSND)),
-            dma((PIECES, NSND)),
-            dma((PIECES, NSND)),
-            dma((PIECES, NSND)),
-            dma((PIECES, NTILE)),
-            dma((PIECES, NTILE)),
-            dma((PIECES, NSND)),
-            dma((PIECES, NSND)),
-            dma((NTILE,)),
-            dma((NTILE,)),
-            dma((NSND,)),
-            dma((NSND,)),
+            dma((PIECES,)),
+            dma((PIECES,)),
+            dma((PIECES,)),
+            dma((PIECES,)),
+            dma((PIECES,)),
+            dma((PIECES,)),
+            dma((PIECES,)),
+            dma((PIECES,)),
+            dma((PIECES,)),
+            dma((PIECES,)),
+            dma((PIECES,)),
+            dma((PIECES,)),
+            dma((PIECES,)),
+            dma((PIECES,)),
+            dma((PIECES,)),
+            dma((PIECES,)),
         ],
         compiler_params=pltpu.CompilerParams(
             collective_id=0, has_side_effects=True, vmem_limit_bytes=VMEM_LIMIT

time: 64 us -> 59.1 us (0.923)
  Pallas kernels: 62.3 us -> 57.6 us
    pallas_call x1, Pallas kernels: 59.9 us -> 55.2 us  [shards(): pl.pallas_call(kernel, out_shape=(jax.ShapeDtypeStruct((TDEV, TOP), f32),...]
where the time goes in v4:
time: 59.1 us; the launch traced here: 58.3 us
  Pallas kernels  57.6 us (97%)
  between operations  0.64 us (1%)
    pallas_call x1, Pallas kernels, shards(): pl.pallas_call(kernel, out_shape=(jax.ShapeDtypeStruct((TDEV, TOP), f32),...  55.2 us
    pallas_call x1, Pallas kernels, shards(): pl.pallas_call(finish, out_shape=(out, out), in_specs=[anywhere, anywhere...  2.42 us

profile of v4, /device:TPU:0, one launch (start us, length us, event | category | flops | bytes accessed | tf_op | source)
XLA Modules:
  0.0 58.3 jit_solution(1238892469508381762)
XLA Ops:
  0.6 55.2 %shard_map.68 = (f32[8,12288]{1,0:T(8,128)}, f32[8,128]{1,0:T(8,128)}) custom-call(s32[1,16]{1,0:T(1,128)} %footprints.1, s32[128]{0:T(128)} %tile_home.1, f32[8,30720]{1,0:T(8,128)} %level_set.3, bf16[1,48,4096]{2,1,0:T(8,128)(2,1)} %adjoint_source.1, bf16[1,3,48,4096]{3,2,1,0:T(8,128)(2,1)} %primal_fields.1), custom_call_target="tpu_custom_call" | custom-call | tf_op jit(solution)/shard_map/pallas_call | solution.py:505
  55.8 2.4 %shard_map.69 = (f32[8,30720]{1,0:T(8,128)}, f32[8,30720]{1,0:T(8,128)}) custom-call(f32[8,12288]{1,0:T(8,128)} %get-tuple-element.4.grad, f32[8,128]{1,0:T(8,128)} %get-tuple-element.5.peak, f32[8,30720]{1,0:T(8,128)} %level_set.3), custom_call_target="tpu_custom_call" | custom-call | tf_op jit(solution)/shard_map/pallas_call | solution.py:559

commit v5 on v4

--- a/solution.py
+++ b/solution.py
@@ -22,11 +22,36 @@
 SLAB = TOP // NSND
 CHUNKS = SLAB // 128
 SROWS = CHUNKS * ENTRIES
-DEPTHS = (8, 8, 8, 8, 8, 8)
-PIECES = len(DEPTHS)
-FIRST = [sum(DEPTHS[:p]) for p in range(PIECES)]
-PCHUNKS = [d // 4 for d in DEPTHS]
-MOST = max(PCHUNKS)
+
+
+class Pieces:
+    def __init__(self, depths):
+        self.depths = depths
+        self.count = len(depths)
+        self.first = [sum(depths[:p]) for p in range(self.count)]
+        self.chunks = [d // 4 for d in depths]
+        self.most = max(self.chunks)
+
+    def within(self, p):
+        return pl.ds(0, self.chunks[p] * 128)
+
+    def cells(self, p, k):
+        size = self.chunks[p] * 128
+        return pl.ds(pl.multiple_of(self.first[p] * TX * TX + k * size, 128), size)
+
+    def rows(self, p, k):
+        size = self.chunks[p] * ENTRIES
+        return pl.ds(pl.multiple_of(self.first[p] * 2 * ENTRIES + k * size, ENTRIES), size)
+
+    def seven(self, p):
+        return pl.ds(0, 7 * self.chunks[p] * ENTRIES)
+
+    def steps(self, p):
+        return self.first[p] // 2, (self.first[p] + self.depths[p]) // 2
+
+
+FETCH = Pieces((8, 8, 8, 8, 8, 8))
+GIVE = Pieces((8, 8, 8, 8, 8, 8))
 
 PLANE = ((2, 2), (1, 2), (3, 2), (2, 1), (2, 3), (1, 1), (3, 3), (1, 3), (3, 1), (0, 2), (2, 0), (0, 1), (0, 3), (1, 0), (3, 0))
 COLUMN = ((2, 1), (2, 0), (1, 1), (3, 1), (1, 0), (3, 0), (0, 1))
@@ -48,38 +73,13 @@
     return [pltpu.roll(turned[(8 - q) % 8], 128 - TX * q, 1) if q else turned[0] for q in range(8)]
 
 
-def split3(x):
+def split2(x):
     hi = x.astype(jnp.bfloat16)
-    rest = x - hi.astype(jnp.float32)
-    mid = rest.astype(jnp.bfloat16)
-    lo = (rest - mid.astype(jnp.float32)).astype(jnp.bfloat16)
-    return hi, mid, lo
+    return hi, (x - hi.astype(jnp.float32)).astype(jnp.bfloat16)
 
 
 def onehot_dot(onehot, x):
-    return sum(jnp.dot(onehot, part, preferred_element_type=jnp.float32) for part in split3(x))
-
-
-def within(p):
-    return pl.ds(0, PCHUNKS[p] * 128)
-
-
-def piece_cells(p, k):
-    size = PCHUNKS[p] * 128
-    return pl.ds(pl.multiple_of(FIRST[p] * TX * TX + k * size, 128), size)
-
-
-def piece_rows(p, k):
-    size = PCHUNKS[p] * ENTRIES
-    return pl.ds(pl.multiple_of(FIRST[p] * 2 * ENTRIES + k * size, ENTRIES), size)
-
-
-def piece_seven(p):
-    return pl.ds(0, 7 * PCHUNKS[p] * ENTRIES)
-
-
-def piece_steps(p):
-    return FIRST[p] // 2, (FIRST[p] + DEPTHS[p]) // 2
+    return sum(jnp.dot(onehot, part, preferred_element_type=jnp.float32) for part in split2(x))
 
 
 def kernel(
@@ -149,16 +149,16 @@
         pl.semaphore_signal(barrier, inc=1, device_id=(to, tile), device_id_type=MESH)
 
     own = []
-    for p in range(PIECES):
-        cells = piece_cells(p, snd)
+    for p in range(FETCH.count):
+        cells = FETCH.cells(p, snd)
         own.append(
             pltpu.make_async_copy(
-                level_set.at[:, cells], gathered.at[p, tile, :, within(p)], local_sem.at[p]
+                level_set.at[:, cells], gathered.at[p, tile, :, FETCH.within(p)], local_sem.at[p]
             )
         )
         own[-1].start()
-    load_src = pltpu.make_async_copy(adjoint_source, src_in, local_sem.at[PIECES])
-    load_prim = pltpu.make_async_copy(primal_fields, prim_in, local_sem.at[PIECES + 1])
+    load_src = pltpu.make_async_copy(adjoint_source, src_in, local_sem.at[FETCH.count])
+    load_prim = pltpu.make_async_copy(primal_fields, prim_in, local_sem.at[FETCH.count + 1])
     load_src.start()
     load_prim.start()
 
@@ -194,14 +194,14 @@
     pl.semaphore_wait(barrier, 22)
 
     ag = []
-    for p in range(PIECES):
-        block = gathered.at[p, tile, :, within(p)]
+    for p in range(FETCH.count):
+        block = gathered.at[p, tile, :, FETCH.within(p)]
         ag.append(
             send_all(
                 [(block, block, (snd, to)) for to in plane],
                 ag_send.at[p],
                 ag_recv.at[p],
-                gathered.at[p, 0:15, :, within(p)],
+                gathered.at[p, 0:15, :, FETCH.within(p)],
             )
         )
         if p == 0:
@@ -264,24 +264,24 @@
     place = onehot.T.astype(jnp.bfloat16)
     gather_sends = len(sends)
     pk = []
-    for p in range(PIECES):
+    for p in range(FETCH.count):
         wait_all(ag[p])
-        for c in range(PCHUNKS[p]):
+        for c in range(FETCH.chunks[p]):
             cells = gathered[p, :, :, c * 128 : (c + 1) * 128].reshape(TILES, 128)
             picked[p, :, c * ENTRIES : (c + 1) * ENTRIES, :] = onehot_dot(pick, cells).reshape(
                 NSND, ENTRIES, 128
             )
-        rows = piece_rows(p, snd)
-        size = PCHUNKS[p] * ENTRIES
+        rows = FETCH.rows(p, snd)
+        size = FETCH.chunks[p] * ENTRIES
         pk.append(
             send_all(
                 [(picked.at[p, to, 0:size], returned.at[rows], (to, tile)) for to in column],
                 pk_send.at[p],
                 pk_recv.at[p],
-                returned.at[piece_seven(p)],
-            )
-        )
-        returned[rows, :] = picked[p, snd, 0 : PCHUNKS[p] * ENTRIES]
+                returned.at[FETCH.seven(p)],
+            )
+        )
+        returned[rows, :] = picked[p, snd, 0 : FETCH.chunks[p] * ENTRIES]
 
     drain(gather_sends)
 
@@ -312,9 +312,9 @@
             va[row + q + 1, pl.ds(depth + 8, 8), :] = source[row + q, at, :] * inv
         return carry
 
-    for p in range(PIECES):
+    for p in range(FETCH.count):
         wait_all(pk[p])
-        lax.fori_loop(*piece_steps(p), enter, 0, unroll=min(8, DEPTHS[p] // 2))
+        lax.fori_loop(*FETCH.steps(p), enter, 0, unroll=min(8, FETCH.depths[p] // 2))
 
     def sweep(now, keep):
         now[0, 8:56, :] = jnp.where(left, 0.0, pltpu.roll(now[32, 8:56, :], 64, 1))
@@ -370,13 +370,13 @@
 
     pick_sends = len(sends)
     og = []
-    for p in range(PIECES):
-        lax.fori_loop(*piece_steps(p), leave, 0, unroll=min(8, DEPTHS[p] // 2))
-        size = PCHUNKS[p] * ENTRIES
+    for p in range(GIVE.count):
+        lax.fori_loop(*GIVE.steps(p), leave, 0, unroll=min(8, GIVE.depths[p] // 2))
+        size = GIVE.chunks[p] * ENTRIES
         og.append(
             send_all(
                 [
-                    (outgoing.at[piece_rows(p, to)], arrived.at[p, snd, 0:size], (to, tile))
+                    (outgoing.at[GIVE.rows(p, to)], arrived.at[p, snd, 0:size], (to, tile))
                     for to in column
                 ],
                 og_send.at[p],
@@ -384,16 +384,16 @@
                 arrived.at[p, 0:7, 0:size],
             )
         )
-        rows = piece_rows(p, snd)
-        arrived[p, snd, 0 : PCHUNKS[p] * ENTRIES] = outgoing[rows, :]
+        rows = GIVE.rows(p, snd)
+        arrived[p, snd, 0 : GIVE.chunks[p] * ENTRIES] = outgoing[rows, :]
 
     drain(pick_sends)
 
     og_sends = len(sends)
     rs = []
-    for p in range(PIECES):
+    for p in range(GIVE.count):
         wait_all(og[p])
-        for c in range(PCHUNKS[p]):
+        for c in range(GIVE.chunks[p]):
             cells = arrived[p, :, c * ENTRIES : (c + 1) * ENTRIES, :].reshape(TILES, 128)
             partial[p, :, :, c * 128 : (c + 1) * 128] = onehot_dot(place, cells).reshape(
                 NTILE, TDEV, 128
@@ -401,32 +401,32 @@
         rs.append(
             send_all(
                 [
-                    (partial.at[p, to, :, within(p)], owned.at[p, tile, :, within(p)], (snd, to))
+                    (partial.at[p, to, :, GIVE.within(p)], owned.at[p, tile, :, GIVE.within(p)], (snd, to))
                     for to in plane
                 ],
                 rs_send.at[p],
                 rs_recv.at[p],
-                owned.at[p, 0:15, :, within(p)],
-            )
-        )
-        owned[p, tile, :, within(p)] = partial[p, tile, :, within(p)]
+                owned.at[p, 0:15, :, GIVE.within(p)],
+            )
+        )
+        owned[p, tile, :, GIVE.within(p)] = partial[p, tile, :, GIVE.within(p)]
 
     drain(og_sends)
 
     rs_sends = len(sends)
     fin = []
     top = jnp.zeros((TDEV, 128), jnp.float32)
-    for p in range(PIECES):
+    for p in range(GIVE.count):
         wait_all(rs[p])
-        slab = owned[p, 0, :, within(p)]
+        slab = owned[p, 0, :, GIVE.within(p)]
         for i in range(1, NTILE):
-            slab = slab + owned[p, i, :, within(p)]
-        cells = piece_cells(p, snd)
+            slab = slab + owned[p, i, :, GIVE.within(p)]
+        cells = GIVE.cells(p, snd)
         grad_ref[:, cells] = slab
         size = jnp.abs(slab)
-        for c in range(PCHUNKS[p]):
+        for c in range(GIVE.chunks[p]):
             top = jnp.maximum(top, size[:, c * 128 : (c + 1) * 128])
-        if p == PIECES - 1:
+        if p == GIVE.count - 1:
             peaks[tile] = jnp.max(top, axis=0, keepdims=True)
             peak = peaks.at[tile]
             mp = send_all(
@@ -441,7 +441,7 @@
                 [(block, block, (to, tile)) for to in column],
                 fin_send.at[p],
                 fin_recv.at[p],
-                grad_ref.at[:, pl.ds(0, 7 * PCHUNKS[p] * 128)],
+                grad_ref.at[:, pl.ds(0, 7 * GIVE.chunks[p] * 128)],
             )
         )
 
@@ -513,9 +513,9 @@
         scratch_shapes=[
             pltpu.VMEM(adjoint_source.shape, jnp.bfloat16),
             pltpu.VMEM(primal_fields.shape, jnp.bfloat16),
-            pltpu.VMEM((PIECES, NTILE, TDEV, MOST * 128), f32),
+            pltpu.VMEM((FETCH.count, NTILE, TDEV, FETCH.most * 128), f32),
             pltpu.VMEM((NSND * ENTRIES, TILES), f32),
-            pltpu.VMEM((PIECES, NSND, MOST * ENTRIES, 128), f32),
+            pltpu.VMEM((FETCH.count, NSND, FETCH.most * ENTRIES, 128), f32),
             pltpu.VMEM((NSND * SROWS, 128), f32),
             field,
             field,
@@ -527,29 +527,29 @@
             padded,
             field,
             pltpu.VMEM((NSND * SROWS, 128), f32),
-            pltpu.VMEM((PIECES, NSND, MOST * ENTRIES, 128), f32),
-            pltpu.VMEM((PIECES, NTILE, TDEV, MOST * 128), f32),
-            pltpu.VMEM((PIECES, NTILE, TDEV, MOST * 128), f32),
+            pltpu.VMEM((GIVE.count, NSND, GIVE.most * ENTRIES, 128), f32),
+            pltpu.VMEM((GIVE.count, NTILE, TDEV, GIVE.most * 128), f32),
+            pltpu.VMEM((GIVE.count, NTILE, TDEV, GIVE.most * 128), f32),
             pltpu.VMEM((NTILE, 1, 128), f32),
             pltpu.VMEM((NSND, 1, 128), f32),
             pltpu.VMEM((TDEV, TOP), f32),
-            dma((PIECES + 2,)),
-            dma((PIECES,)),
-            dma((PIECES,)),
-            dma((PIECES,)),
-            dma((PIECES,)),
-            dma((PIECES,)),
-            dma((PIECES,)),
-            dma((PIECES,)),
-            dma((PIECES,)),
-            dma((PIECES,)),
-            dma((PIECES,)),
-            dma((PIECES,)),
-            dma((PIECES,)),
-            dma((PIECES,)),
-            dma((PIECES,)),
-            dma((PIECES,)),
-            dma((PIECES,)),
+            dma((FETCH.count + 2,)),
+            dma((FETCH.count,)),
+            dma((FETCH.count,)),
+            dma((FETCH.count,)),
+            dma((FETCH.count,)),
+            dma((FETCH.count,)),
+            dma((FETCH.count,)),
+            dma((GIVE.count,)),
+            dma((GIVE.count,)),
+            dma((GIVE.count,)),
+            dma((GIVE.count,)),
+            dma((GIVE.count,)),
+            dma((GIVE.count,)),
+            dma((GIVE.count,)),
+            dma((GIVE.count,)),
+            dma((GIVE.count,)),
+            dma((GIVE.count,)),
         ],
         compiler_params=pltpu.CompilerParams(
             collective_id=0, has_side_effects=True, vmem_limit_bytes=VMEM_LIMIT

time: 59.1 us -> 59.1 us (level)
  no operation moved by 1% of the time
where the time goes in v5:
time: 59.1 us; the launch traced here: 58.2 us
  Pallas kernels  57.6 us (97%)
  between operations  0.64 us (1%)
    pallas_call x1, Pallas kernels, shards(): pl.pallas_call(kernel, out_shape=(jax.ShapeDtypeStruct((TDEV, TOP), f32),...  55.2 us
    pallas_call x1, Pallas kernels, shards(): pl.pallas_call(finish, out_shape=(out, out), in_specs=[anywhere, anywhere...  2.42 us

profile of v5, /device:TPU:0, one launch (start us, length us, event | category | flops | bytes accessed | tf_op | source)
XLA Modules:
  0.0 58.2 jit_solution(7252712374192784550)
XLA Ops:
  0.6 55.2 %shard_map.68 = (f32[8,12288]{1,0:T(8,128)}, f32[8,128]{1,0:T(8,128)}) custom-call(s32[1,16]{1,0:T(1,128)} %footprints.1, s32[128]{0:T(128)} %tile_home.1, f32[8,30720]{1,0:T(8,128)} %level_set.3, bf16[1,48,4096]{2,1,0:T(8,128)(2,1)} %adjoint_source.1, bf16[1,3,48,4096]{3,2,1,0:T(8,128)(2,1)} %primal_fields.1), custom_call_target="tpu_custom_call" | custom-call | tf_op jit(solution)/shard_map/pallas_call | solution.py:505
  55.8 2.4 %shard_map.69 = (f32[8,30720]{1,0:T(8,128)}, f32[8,30720]{1,0:T(8,128)}) custom-call(f32[8,12288]{1,0:T(8,128)} %get-tuple-element.4.grad, f32[8,128]{1,0:T(8,128)} %get-tuple-element.5.peak, f32[8,30720]{1,0:T(8,128)} %level_set.3), custom_call_target="tpu_custom_call" | custom-call | tf_op jit(solution)/shard_map/pallas_call | solution.py:559
